TPU v7x, 32 devices: a whole 2x2x4 slice. The times are simulated.
32 devices in a mesh: replica: 2 (over x), fsdp: 8 (over z, core), tensor: 2 (over y).
Axes of the slice: x: 2, y: 2, z: 4, core: 2. Of those that a mesh axis runs over, the one named last changes fastest.
Arguments:
- inputs: bfloat16 [4096, 1024], P(('replica', 'fsdp')), may hold values from -6 to 6
- cotangent: bfloat16 [4096, 1024], P(('replica', 'fsdp')), may hold values from -6 to 6
- norm_gains: bfloat16 [2, 1024], P(None, 'fsdp'), may hold values from 0.25 to 1.75
- head_gains: bfloat16 [2, 64], P(None, 'fsdp'), may hold values from 0.25 to 1.75
- query_weight: bfloat16 [1024, 1024], P('fsdp', 'tensor'), may hold values from -0.1875 to 0.1875
- key_weight: bfloat16 [1024, 512], P('fsdp', 'tensor'), may hold values from -0.1875 to 0.1875
- value_weight: bfloat16 [1024, 512], P('fsdp', 'tensor'), may hold values from -0.1875 to 0.1875
- out_weight: bfloat16 [1024, 1024], P('tensor', 'fsdp'), may hold values from -1 to 1
- gate_weight: bfloat16 [1024, 4608], P('fsdp', 'tensor'), may hold values from -0.1875 to 0.1875
- up_weight: bfloat16 [1024, 4608], P('fsdp', 'tensor'), may hold values from -0.1875 to 0.1875
- down_weight: bfloat16 [4608, 1024], P('tensor', 'fsdp'), may hold values from -0.09375 to 0.09375
Outputs:
- output: bfloat16 [4096, 1024], P(('replica', 'fsdp'))
- input_grad: bfloat16 [4096, 1024], P(('replica', 'fsdp'))
- norm_gains_grad: float32 [2, 1024], P(None, 'fsdp')
- head_gains_grad: float32 [2, 64], P(None, 'fsdp')
- query_grad: float32 [1024, 1024], P('fsdp', 'tensor')
- key_grad: float32 [1024, 512], P('fsdp', 'tensor')
- value_grad: float32 [1024, 512], P('fsdp', 'tensor')
- out_grad: float32 [1024, 1024], P('tensor', 'fsdp')
- gate_grad: float32 [1024, 4608], P('fsdp', 'tensor')
- up_grad: float32 [1024, 4608], P('fsdp', 'tensor')
- down_grad: float32 [4608, 1024], P('tensor', 'fsdp')
All inputs are finite; a program needn't handle non-finite values.
Results may differ from a plain program's by a relative error of at most 0.02.
Values may be sent and summed in bfloat16 or wider, within the bound.
A program may use at most 128 MiB of HBM per device.

v0:
```python
import math

import jax
import jax.numpy as jnp
from jax import lax
from jax.sharding import PartitionSpec as P

HD = 64


epsilon = 1e-05
rope_base = 1000000.0


def inverse_rms(values):
    return lax.rsqrt(jnp.mean(values * values, axis=-1, keepdims=True) + epsilon)


def norm_back(grad_normed, normed, scaling, gain):
    scaled = grad_normed * gain
    return scaling * (scaled - normed * jnp.mean(scaled * normed, axis=-1, keepdims=True))


def rope_tables(length):
    half = HD // 2
    freqs = rope_base ** (-(jnp.arange(half, dtype=jnp.float32) * 2.0 / HD))
    angles = jnp.arange(length, dtype=jnp.float32)[:, None] * freqs[None, :]
    return (jnp.cos(angles)[:, None, :], jnp.sin(angles)[:, None, :])


def rotate(values, cosine_table, sine_table):
    half = values.shape[-1] // 2
    front = values[..., :half]
    behind = values[..., half:]
    return jnp.concatenate(
        [front * cosine_table - behind * sine_table, behind * cosine_table + front * sine_table],
        axis=-1,
    )


def matmul(left, right):
    return jnp.dot(left, right, preferred_element_type=jnp.float32)


def cross_rows(left, right):
    return lax.dot_general(
        left, right, (((0,), (0,)), ((), ())), preferred_element_type=jnp.float32
    )


def cross_cols(left, right):
    return lax.dot_general(
        left, right, (((1,), (1,)), ((), ())), preferred_element_type=jnp.float32
    )


def local(
    inputs,
    cotangent,
    norm_gains,
    head_gains,
    query_weight,
    key_weight,
    value_weight,
    out_weight,
    gate_weight,
    up_weight,
    down_weight,
):
    length = inputs.shape[0]
    gains_full, heads_full, query_full, key_full, value_full, out_full = (
        lax.all_gather(norm_gains, "fsdp", axis=1, tiled=True),
        lax.all_gather(head_gains, "fsdp", axis=1, tiled=True),
        lax.all_gather(query_weight, "fsdp", axis=0, tiled=True),
        lax.all_gather(key_weight, "fsdp", axis=0, tiled=True),
        lax.all_gather(value_weight, "fsdp", axis=0, tiled=True),
        lax.all_gather(out_weight, "fsdp", axis=1, tiled=True),
    )
    cosine_table, sine_table = rope_tables(length)
    local_heads = query_full.shape[1] // HD
    local_groups = key_full.shape[1] // HD
    group_size = local_heads // local_groups
    block_rows = min(length, 512)
    score_scale = 1.0 / math.sqrt(HD)
    residual_in = inputs.astype(jnp.float32)
    first_scale = inverse_rms(residual_in)
    first_hat = residual_in * first_scale
    first_gain = gains_full[0].astype(jnp.float32)
    first_low = (first_hat * first_gain).astype(jnp.bfloat16)
    query_raw = matmul(first_low, query_full).reshape(length, local_heads, HD)
    key_raw = matmul(first_low, key_full).reshape(length, local_groups, HD)
    value_low = matmul(first_low, value_full).astype(jnp.bfloat16).reshape(length, local_groups, HD)
    query_gain = heads_full[0].astype(jnp.float32)
    key_gain = heads_full[1].astype(jnp.float32)
    query_scale = inverse_rms(query_raw)
    query_hat = query_raw * query_scale
    query_low = rotate(query_hat * query_gain, cosine_table, sine_table).astype(jnp.bfloat16)
    query_low = query_low.reshape(length, local_groups, group_size, HD)
    key_scale = inverse_rms(key_raw)
    key_hat = key_raw * key_scale
    key_low = rotate(key_hat * key_gain, cosine_table, sine_table).astype(jnp.bfloat16)

    def masked_scores(block_start):
        key_span = block_start + block_rows
        scores = (
            jnp.einsum("qkgd,tkd->kgqt", query_low, key_low, preferred_element_type=jnp.float32)
            * score_scale
        )
        causal = (block_start + jnp.arange(block_rows))[:, None] >= jnp.arange(key_span)[None, :]
        return jnp.where(causal, scores, -1e30)

    block_index = 0
    block_start = block_index * block_rows
    masked = masked_scores(block_start)
    highest = jnp.max(masked, axis=-1, keepdims=True)
    powers = jnp.exp(masked - highest)
    totals = jnp.sum(powers, axis=-1, keepdims=True)
    softmax_low = (powers / totals).astype(jnp.bfloat16)
    log_totals = [highest + jnp.log(totals)]
    mixed_parts = jnp.einsum(
        "kgqt,tkd->qkgd", softmax_low, value_low, preferred_element_type=jnp.float32
    )
    mixed_low = mixed_parts.astype(jnp.bfloat16).reshape(length, local_heads * HD)
    attention_total = lax.psum(matmul(mixed_low, out_full), "tensor")
    hidden = residual_in + attention_total
    gate_full, up_full, down_full = (
        lax.all_gather(gate_weight, "fsdp", axis=0, tiled=True),
        lax.all_gather(up_weight, "fsdp", axis=0, tiled=True),
        lax.all_gather(down_weight, "fsdp", axis=1, tiled=True),
    )
    second_scale = inverse_rms(hidden)
    second_hat = hidden * second_scale
    second_gain = gains_full[1].astype(jnp.float32)
    second_low = (second_hat * second_gain).astype(jnp.bfloat16)
    gate_value = matmul(second_low, gate_full)
    up_value = matmul(second_low, up_full)
    sigmoid_gate = jax.nn.sigmoid(gate_value)
    swish = gate_value * sigmoid_gate
    inner_low = (swish * up_value).astype(jnp.bfloat16)
    swiglu_total = lax.psum(matmul(inner_low, down_full).astype(jnp.bfloat16), "tensor").astype(
        jnp.float32
    )
    output = (hidden + swiglu_total).astype(jnp.bfloat16)
    gate_back, up_back, down_back = (
        lax.all_gather(gate_weight, "fsdp", axis=0, tiled=True),
        lax.all_gather(up_weight, "fsdp", axis=0, tiled=True),
        lax.all_gather(down_weight, "fsdp", axis=1, tiled=True),
    )
    grad_inner = cross_cols(cotangent, down_back)
    grad_gate = (
        grad_inner * up_value * sigmoid_gate * (1.0 + gate_value * (1.0 - sigmoid_gate))
    ).astype(jnp.bfloat16)
    grad_up = (grad_inner * swish).astype(jnp.bfloat16)
    swiglu_parts = (
        cross_rows(second_low, grad_gate),
        cross_rows(second_low, grad_up),
        cross_rows(inner_low, cotangent),
    )
    gate_grad, up_grad, down_grad = (
        lax.psum_scatter(
            swiglu_parts[0].astype(jnp.bfloat16), "fsdp", scatter_dimension=0, tiled=True
        ).astype(jnp.float32),
        lax.psum_scatter(
            swiglu_parts[1].astype(jnp.bfloat16), "fsdp", scatter_dimension=0, tiled=True
        ).astype(jnp.float32),
        lax.psum_scatter(
            swiglu_parts[2].astype(jnp.bfloat16), "fsdp", scatter_dimension=1, tiled=True
        ).astype(jnp.float32),
    )
    grad_second = lax.psum(
        (cross_cols(grad_gate, gate_back) + cross_cols(grad_up, up_back)).astype(jnp.bfloat16),
        "tensor",
    ).astype(jnp.float32)
    second_gain_grad = jnp.sum(grad_second * second_hat, axis=0)
    grad_hidden = cotangent.astype(jnp.float32) + norm_back(
        grad_second, second_hat, second_scale, second_gain
    )
    grad_hidden_low = grad_hidden.astype(jnp.bfloat16)
    gains_back, heads_back, query_back, key_back, value_back, out_back = (
        lax.all_gather(norm_gains, "fsdp", axis=1, tiled=True),
        lax.all_gather(head_gains, "fsdp", axis=1, tiled=True),
        lax.all_gather(query_weight, "fsdp", axis=0, tiled=True),
        lax.all_gather(key_weight, "fsdp", axis=0, tiled=True),
        lax.all_gather(value_weight, "fsdp", axis=0, tiled=True),
        lax.all_gather(out_weight, "fsdp", axis=1, tiled=True),
    )
    out_part = cross_rows(mixed_low, grad_hidden_low)
    grad_mixed = (
        cross_cols(grad_hidden_low, out_back)
        .astype(jnp.bfloat16)
        .reshape(length, local_groups, group_size, HD)
    )
    grad_keys = jnp.zeros((length, local_groups, HD), jnp.float32)
    grad_values = jnp.zeros((length, local_groups, HD), jnp.float32)
    block_index = 0
    block_start = block_index * block_rows
    key_span = block_start + block_rows
    masked = masked_scores(block_start)
    powers = jnp.exp(masked - log_totals[block_index])
    grad_powers = jnp.einsum(
        "qkgd,tkd->kgqt", grad_mixed, value_low, preferred_element_type=jnp.float32
    )
    centred = jnp.sum(powers * grad_powers, axis=-1, keepdims=True)
    grad_scores = (powers * (grad_powers - centred)).astype(jnp.bfloat16)
    query_parts = (
        jnp.einsum("kgqt,tkd->qkgd", grad_scores, key_low, preferred_element_type=jnp.float32)
        * score_scale
    )
    grad_keys = grad_keys.at[:key_span].add(
        jnp.einsum("kgqt,qkgd->tkd", grad_scores, query_low, preferred_element_type=jnp.float32)
        * score_scale
    )
    grad_values = grad_values.at[:key_span].add(
        jnp.einsum(
            "kgqt,qkgd->tkd",
            powers.astype(jnp.bfloat16),
            grad_mixed,
            preferred_element_type=jnp.float32,
        )
    )
    grad_query_rot = query_parts.reshape(length, local_heads, HD)
    grad_query_gained = rotate(grad_query_rot, cosine_table, -sine_table)
    query_gain_grad = jnp.sum(grad_query_gained * query_hat, axis=(0, 1))
    grad_query = norm_back(grad_query_gained, query_hat, query_scale, query_gain).astype(
        jnp.bfloat16
    )
    grad_query = grad_query.reshape(length, local_heads * HD)
    grad_key_gained = rotate(grad_keys, cosine_table, -sine_table)
    key_gain_grad = jnp.sum(grad_key_gained * key_hat, axis=(0, 1))
    grad_key = norm_back(grad_key_gained, key_hat, key_scale, key_gain).astype(jnp.bfloat16)
    grad_key = grad_key.reshape(length, local_groups * HD)
    grad_value = grad_values.astype(jnp.bfloat16).reshape(length, local_groups * HD)
    query_part = cross_rows(first_low, grad_query)
    key_part = cross_rows(first_low, grad_key)
    value_part = cross_rows(first_low, grad_value)
    first_part = (
        cross_cols(grad_query, query_back)
        + cross_cols(grad_key, key_back)
        + cross_cols(grad_value, value_back)
    )
    grad_first, head_part = (
        lax.psum(first_part.astype(jnp.bfloat16), "tensor").astype(jnp.float32),
        lax.psum(jnp.stack([query_gain_grad, key_gain_grad]).astype(jnp.bfloat16), "tensor").astype(
            jnp.float32
        ),
    )
    first_gain_grad = jnp.sum(grad_first * first_hat, axis=0)
    input_grad = (grad_hidden + norm_back(grad_first, first_hat, first_scale, first_gain)).astype(
        jnp.bfloat16
    )
    gains_part = jnp.stack([first_gain_grad, second_gain_grad])
    gains_grad, heads_grad, query_grad, key_grad, value_grad, out_grad = (
        lax.psum_scatter(
            gains_part.astype(jnp.bfloat16), "fsdp", scatter_dimension=1, tiled=True
        ).astype(jnp.float32),
        lax.psum_scatter(
            head_part.astype(jnp.bfloat16), "fsdp", scatter_dimension=1, tiled=True
        ).astype(jnp.float32),
        lax.psum_scatter(
            query_part.astype(jnp.bfloat16), "fsdp", scatter_dimension=0, tiled=True
        ).astype(jnp.float32),
        lax.psum_scatter(
            key_part.astype(jnp.bfloat16), "fsdp", scatter_dimension=0, tiled=True
        ).astype(jnp.float32),
        lax.psum_scatter(
            value_part.astype(jnp.bfloat16), "fsdp", scatter_dimension=0, tiled=True
        ).astype(jnp.float32),
        lax.psum_scatter(
            out_part.astype(jnp.bfloat16), "fsdp", scatter_dimension=1, tiled=True
        ).astype(jnp.float32),
    )
    summed = (
        lax.psum(gains_grad.astype(jnp.bfloat16), "replica").astype(jnp.float32),
        lax.psum(heads_grad.astype(jnp.bfloat16), "replica").astype(jnp.float32),
        lax.psum(query_grad.astype(jnp.bfloat16), "replica").astype(jnp.float32),
        lax.psum(key_grad.astype(jnp.bfloat16), "replica").astype(jnp.float32),
        lax.psum(value_grad.astype(jnp.bfloat16), "replica").astype(jnp.float32),
        lax.psum(out_grad.astype(jnp.bfloat16), "replica").astype(jnp.float32),
        lax.psum(gate_grad.astype(jnp.bfloat16), "replica").astype(jnp.float32),
        lax.psum(up_grad.astype(jnp.bfloat16), "replica").astype(jnp.float32),
        lax.psum(down_grad.astype(jnp.bfloat16), "replica").astype(jnp.float32),
    )
    return (
        output,
        input_grad,
        summed[0],
        summed[1],
        summed[2],
        summed[3],
        summed[4],
        summed[5],
        summed[6],
        summed[7],
        summed[8],
    )


def solution(mesh):
    return jax.shard_map(
        local,
        mesh=mesh,
        in_specs=(
            P(("replica", "fsdp"), None),
            P(("replica", "fsdp"), None),
            P(None, "fsdp"),
            P(None, "fsdp"),
            P("fsdp", "tensor"),
            P("fsdp", "tensor"),
            P("fsdp", "tensor"),
            P("tensor", "fsdp"),
            P("fsdp", "tensor"),
            P("fsdp", "tensor"),
            P("tensor", "fsdp"),
        ),
        out_specs=(
            P(("replica", "fsdp"), None),
            P(("replica", "fsdp"), None),
            P(None, "fsdp"),
            P(None, "fsdp"),
            P("fsdp", "tensor"),
            P("fsdp", "tensor"),
            P("fsdp", "tensor"),
            P("tensor", "fsdp"),
            P("fsdp", "tensor"),
            P("fsdp", "tensor"),
            P("tensor", "fsdp"),
        ),
        check_vma=False,
    )
```

profile of v0, /device:TPU:16, one launch (start us, length us, event | category | flops | bytes accessed | tf_op | source)
XLA Modules:
  0.0 781.4 jit_solution(12577375317862822714)
XLA Ops:
  9.4 9.1 %all_gather.34 = bf16[2,1024]{1,0:T(2,128)(2,1)S(1)} all-gather(bf16[2,128]{1,0:T(2,128)(2,1)} %param.21), channel_id=1, replica_groups=mesh['replica'=2,'fsdp'=8,'tensor'=2] {'fsdp'}, dimensions={1}, use_global_device_ids=true | all-gather | bytes 4608 | tf_op jit(solution)/shard_map/all_gather | solution.py:72
  19.8 8.8 %all-gather = bf16[8,8,2]{1,2,0:T(2,128)(2,1)S(1)} all-gather(bf16[1,8,2]{1,2,0:T(2,128)(2,1)} %bitcast.194), channel_id=1, replica_groups=mesh['replica'=2,'fsdp'=8,'tensor'=2] {'fsdp'}, dimensions={0}, use_global_device_ids=true | all-gather | bytes 288 | tf_op jit(solution)/shard_map/all_gather | solution.py:73
  29.0 16.3 %all_gather.36 = bf16[1024,256]{1,0:T(8,128)(2,1)S(1)} all-gather(bf16[128,256]{1,0:T(8,128)(2,1)} %param.24), channel_id=1, replica_groups=mesh['replica'=2,'fsdp'=8,'tensor'=2] {'fsdp'}, dimensions={0}, use_global_device_ids=true | all-gather | bytes 589824 | tf_op jit(solution)/shard_map/all_gather | solution.py:75
  47.0 15.2 %all_gather.35 = bf16[1024,256]{1,0:T(8,128)(2,1)S(1)} all-gather(bf16[128,256]{1,0:T(8,128)(2,1)S(1)} %copy-done.42), channel_id=1, replica_groups=mesh['replica'=2,'fsdp'=8,'tensor'=2] {'fsdp'}, dimensions={0}, use_global_device_ids=true | all-gather | bytes 589824 | tf_op jit(solution)/shard_map/all_gather | solution.py:76
  68.8 2.7 fusion.51
  74.8 39.0 %all-reduce.9.cloned.1.call-done = f32[256,1024]{1,0:T(8,128)} async-done(((f32[256,1024]{1,0:T(8,128)}), f32[256,1024]{1,0:T(8,128)}) %all-reduce.9.cloned.1.call-update) | async-done | bytes 1048592 | tf_op jit(solution)/shard_map/psum | solution.py:124
  116.4 49.6 %all-gather.11.cloned.1.call-done = bf16[1024,2304]{1,0:T(8,128)(2,1)} async-done(((bf16[128,2304]{1,0:T(8,128)(2,1)}), bf16[1024,2304]{1,0:T(8,128)(2,1)}) %all-gather.11.cloned.1.call-update) | async-done | bytes 4718608 | tf_op jit(solution)/shard_map/all_gather | solution.py:127
  166.0 5.3 fusion.52
  171.3 46.9 %all-gather.13.cloned.1.call-done = bf16[1024,2304]{1,0:T(8,128)(2,1)} async-done(((bf16[128,2304]{1,0:T(8,128)(2,1)}), bf16[1024,2304]{1,0:T(8,128)(2,1)}) %all-gather.13.cloned.1.call-update) | async-done | bytes 4718608 | tf_op jit(solution)/shard_map/all_gather | solution.py:128
  218.1 5.3 fusion.53
  223.4 46.6 %all-gather.15.cloned.1.call-done = bf16[2304,1024]{1,0:T(8,128)(2,1)} async-done(((bf16[2304,128]{1,0:T(8,128)(2,1)}), bf16[2304,1024]{1,0:T(8,128)(2,1)}) %all-gather.15.cloned.1.call-update) | async-done | bytes 4718608 | tf_op jit(solution)/shard_map/all_gather | solution.py:129
  270.1 7.1 multiply_convert_fusion
  277.2 4.6 fusion.54
  287.4 4.9 convolution_convert_fusion.7
  292.3 20.6 %all-reduce.11.cloned.1.call-done = bf16[256,1024]{1,0:T(8,128)(2,1)} async-done(((bf16[256,1024]{1,0:T(8,128)(2,1)}), bf16[256,1024]{1,0:T(8,128)(2,1)}) %all-reduce.11.cloned.1.call-update) | async-done | bytes 524304 | tf_op jit(solution)/shard_map/psum | solution.py:170
  332.6 5.0 convolution_convert_fusion
  337.6 6.7 copy.84
  349.6 4.9 convolution_convert_fusion.2
  354.9 4.9 convolution_convert_fusion.1
  360.5 10.6 %all-reduce.13.cloned.1.call-done = (bf16[256,1024]{1,0:T(8,128)(2,1)}, bf16[256,1024]{1,0:T(8,128)(2,1)}) async-done(((bf16[256,1024]{1,0:T(8,128)(2,1)}, bf16[256,1024]{1,0:T(8,128)(2,1)}), (bf16[256,1024]{1,0:T(8,128)(2,1)}, bf16[256,1024]{1,0:T(8,128)(2,1)})) %all-reduce.13.cloned.1.call-update) | async-done | bytes 1048592 | tf_op jit(solution)/shard_map/psum | solution.py:140
  373.6 26.1 %reduce-scatter.28.cloned.1.call-done = bf16[128,512]{1,0:T(8,128)(2,1)} async-done(((bf16[1024,512]{1,0:T(8,128)(2,1)}), bf16[128,512]{1,0:T(8,128)(2,1)}) %reduce-scatter.28.cloned.1.call-update) | async-done | bytes 131088
  401.4 57.4 %reduce-scatter.30.cloned.1.call-done = bf16[128,2304]{1,0:T(8,128)(2,1)} async-done(((bf16[1024,2304]{1,0:T(8,128)(2,1)}), bf16[128,2304]{1,0:T(8,128)(2,1)}) %reduce-scatter.30.cloned.1.call-update) | async-done | bytes 589840
  460.9 26.0 %reduce-scatter.20.cloned.1.call-done = bf16[128,256]{1,0:T(8,128)(2,1)} async-done(((bf16[1024,256]{1,0:T(8,128)(2,1)}), bf16[128,256]{1,0:T(8,128)(2,1)}) %reduce-scatter.20.cloned.1.call-update) | async-done | bytes 65552 | tf_op jit(solution)/shard_map/reduce_scatter | solution.py:265
  486.9 31.3 %reduce-scatter.18.cloned.1.call-done = bf16[128,256]{1,0:T(8,128)(2,1)} async-done(((bf16[1024,256]{1,0:T(8,128)(2,1)}), bf16[128,256]{1,0:T(8,128)(2,1)}) %reduce-scatter.18.cloned.1.call-update) | async-done | bytes 65552 | tf_op jit(solution)/shard_map/reduce_scatter | solution.py:262
  518.1 33.6 %reduce-scatter.16.cloned.1.call-done = bf16[128,512]{1,0:T(8,128)(2,1)} async-done(((bf16[1024,512]{1,0:T(8,128)(2,1)}), bf16[128,512]{1,0:T(8,128)(2,1)}) %reduce-scatter.16.cloned.1.call-update) | async-done | bytes 131088 | tf_op jit(solution)/shard_map/reduce_scatter | solution.py:259
  551.7 58.9 %reduce-scatter.22.cloned.1.call-done = bf16[128,2304]{1,0:T(8,128)(2,1)} async-done(((bf16[1024,2304]{1,0:T(8,128)(2,1)}), bf16[128,2304]{1,0:T(8,128)(2,1)}) %reduce-scatter.22.cloned.1.call-update) | async-done | bytes 589840 | tf_op jit(solution)/shard_map/reduce_scatter | solution.py:160
  610.6 55.6 %reduce-scatter.24.cloned.1.call-done = bf16[128,2304]{1,0:T(8,128)(2,1)} async-done(((bf16[1024,2304]{1,0:T(8,128)(2,1)}), bf16[128,2304]{1,0:T(8,128)(2,1)}) %reduce-scatter.24.cloned.1.call-update) | async-done | bytes 589840 | tf_op jit(solution)/shard_map/reduce_scatter | solution.py:163
  667.7 11.0 %all-reduce = bf16[2,64]{1,0:T(2,128)(2,1)S(1)} all-reduce(bf16[2,64]{1,0:T(2,128)(2,1)S(1)} %pad_maximum_fusion.6), channel_id=3, replica_groups=mesh['replica'=2,'fsdp'=8,'tensor'=2] {'fsdp'}, use_global_device_ids=true, to_apply=%region_24.25.clone | all-reduce | flops 128 | bytes 512
  678.8 4.9 psum.112
  686.8 7.4 reduce-scatter.26.cloned.1.call-done
  695.0 4.9 all-reduce.2
  701.1 66.5 %all-reduce.15.cloned.1.call-done = (bf16[128,512]{1,0:T(8,128)(2,1)}, bf16[128,256]{1,0:T(8,128)(2,1)}, bf16[128,256]{1,0:T(8,128)(2,1)}, bf16[512,128]{1,0:T(8...) async-done(((bf16[128,512]{1,0:T(8,128)(2,1)}, bf16[128,256]{1,0:T(8,128)(2,1)}, bf16[128,256]{1,0:T(8,128)(2,1)}, ...) | async-done | bytes 2162704 | tf_op jit(solution)/shard_map/psum | solution.py:275
  (260 shorter events, 68.0 us)
Async XLA Ops:
  7.2 55.1 %copy-start.3 = (bf16[256,1024]{1,0:T(8,128)(2,1)S(1)}, bf16[256,1024]{1,0:T(8,128)(2,1)}, u32[]{:S(2)}) copy-start(bf16[256,1024]{1,0:T(8,128)(2,1)} %param.19) | copy-start | bytes 1572868
  7.2 39.8 %copy-start.42 = (bf16[128,256]{1,0:T(8,128)(2,1)S(1)}, bf16[128,256]{1,0:T(8,128)(2,1)}, u32[]{:S(2)}) copy-start(bf16[128,256]{1,0:T(8,128)(2,1)} %param.25) | copy-start | bytes 196612
  7.2 56.9 %all-gather.7.cloned.1.call-start = ((), (), s32[]{:S(2)}) async-start(), calls=%async_computation.8 | async-start | bytes 1179648 | tf_op jit(solution)/shard_map/all_gather | solution.py:74
  7.9 60.8 %all-gather.9.cloned.1.call-start = ((), (), s32[]{:S(2)}) async-start(), calls=%async_computation.9 | async-start | bytes 1179648 | tf_op jit(solution)/shard_map/all_gather | solution.py:77
  8.7 105.2 %all-reduce.9.cloned.1.call-start = ((), (), s32[]{:S(2)}) async-start(), calls=%async_computation.10 | async-start | bytes 2097152 | tf_op jit(solution)/shard_map/psum | solution.py:124
  18.5 45.6 %copy-start.48 = (f32[1,1024]{1,0:T(1,128)}, f32[1,1024]{1,0:T(1,128)S(1)}, u32[]{:S(2)}) copy-start(f32[1,1024]{1,0:T(1,128)S(1)} %get-tuple-element.88) | copy-start | bytes 12292
  18.5 96.9 %copy-start.40 = (f32[1,1024]{1,0:T(1,128)}, f32[1,1024]{1,0:T(1,128)S(1)}, u32[]{:S(2)}) copy-start(f32[1,1024]{1,0:T(1,128)S(1)} %get-tuple-element.87) | copy-start | bytes 12292
  19.8 44.3 %copy-start.54 = (f32[256]{0:T(256)}, f32[256]{0:T(256)S(1)}, u32[]{:S(2)}) copy-start(f32[256]{0:T(256)S(1)} %add_rsqrt_fusion.3) | copy-start | bytes 3076
  28.7 34.6 %copy-start.61 = (f32[64]{0:T(128)}, f32[64]{0:T(128)S(1)}, u32[]{:S(2)}) copy-start(f32[64]{0:T(128)S(1)} %get-tuple-element.92) | copy-start | bytes 772
  28.7 37.4 %copy-start.58 = (f32[64]{0:T(128)}, f32[64]{0:T(128)S(1)}, u32[]{:S(2)}) copy-start(f32[64]{0:T(128)S(1)} %get-tuple-element.93) | copy-start | bytes 772
  46.9 16.4 %copy-start.8 = (f32[256,256]{0,1:T(8,128)}, f32[256,256]{0,1:T(8,128)S(1)}, u32[]{:S(2)}) copy-start(f32[256,256]{0,1:T(8,128)S(1)} %get-tuple-element.95) | copy-start | bytes 786436
  47.0 17.1 %copy-start.46 = (f32[256,4]{0,1:T(4,128)}, f32[256,4]{0,1:T(4,128)S(1)}, u32[]{:S(2)}) copy-start(f32[256,4]{0,1:T(4,128)S(1)} %add_rsqrt_fusion.1) | copy-start | bytes 12292
  68.7 4.8 copy-start.62
  68.7 5.4 copy-start.59
  71.5 94.5 %all-gather.11.cloned.1.call-start = ((), (), s32[]{:S(2)}) async-start(), calls=%async_computation.11 | async-start | bytes 5308416 | tf_op jit(solution)/shard_map/all_gather | solution.py:127
  72.1 146.0 %all-gather.13.cloned.1.call-start = ((), (), s32[]{:S(2)}) async-start(), calls=%async_computation.12 | async-start | bytes 5308416 | tf_op jit(solution)/shard_map/all_gather | solution.py:128
  72.7 197.4 %all-gather.15.cloned.1.call-start = ((), (), s32[]{:S(2)}) async-start(), calls=%async_computation.13 | async-start | bytes 5308416 | tf_op jit(solution)/shard_map/all_gather | solution.py:129
  73.3 239.6 %all-reduce.11.cloned.1.call-start = ((), (), s32[]{:S(2)}) async-start(), calls=%async_computation.14 | async-start | bytes 1048576 | tf_op jit(solution)/shard_map/psum | solution.py:170
  284.2 86.9 %all-reduce.13.cloned.1.call-start = ((), (), s32[]{:S(2)}) async-start(), calls=%async_computation.23 | async-start | bytes 2097152 | tf_op jit(solution)/shard_map/psum | solution.py:140
  287.4 25.5 %copy-start.41 = (f32[1,1024]{1,0:T(1,128)S(1)}, f32[1,1024]{1,0:T(1,128)}, u32[]{:S(2)}) copy-start(f32[1,1024]{1,0:T(1,128)} %copy-done.40) | copy-start | bytes 12292
  312.9 4.7 copy-start.7
  330.7 69.0 %reduce-scatter.28.cloned.1.call-start = ((), (), s32[]{:S(2)}) async-start(), calls=%async_computation.21 | async-start | bytes 1179648
  332.6 126.2 %reduce-scatter.30.cloned.1.call-start = ((), (), s32[]{:S(2)}) async-start(), calls=%async_computation.22 | async-start | bytes 5308416
  344.4 142.5 %reduce-scatter.20.cloned.1.call-start = ((), (), s32[]{:S(2)}) async-start(), calls=%async_computation.17 | async-start | bytes 589824 | tf_op jit(solution)/shard_map/reduce_scatter | solution.py:265
  346.7 171.5 %reduce-scatter.18.cloned.1.call-start = ((), (), s32[]{:S(2)}) async-start(), calls=%async_computation.16 | async-start | bytes 589824 | tf_op jit(solution)/shard_map/reduce_scatter | solution.py:262
  348.0 203.7 %reduce-scatter.16.cloned.1.call-start = ((), (), s32[]{:S(2)}) async-start(), calls=%async_computation.15 | async-start | bytes 1179648 | tf_op jit(solution)/shard_map/reduce_scatter | solution.py:259
  349.6 261.0 %reduce-scatter.22.cloned.1.call-start = ((), (), s32[]{:S(2)}) async-start(), calls=%async_computation.18 | async-start | bytes 5308416 | tf_op jit(solution)/shard_map/reduce_scatter | solution.py:160
  354.6 311.6 %reduce-scatter.24.cloned.1.call-start = ((), (), s32[]{:S(2)}) async-start(), calls=%async_computation.19 | async-start | bytes 5308416 | tf_op jit(solution)/shard_map/reduce_scatter | solution.py:163
  359.8 334.4 %reduce-scatter.26.cloned.1.call-start = ((), (), s32[]{:S(2)}) async-start(), calls=%async_computation.20 | async-start | bytes 294912
  372.6 293.6 %copy-start.66 = (u32[32]{0:T(128)S(1)}, u32[32]{0:T(128)}, u32[]{:S(2)}) copy-start(u32[32]{0:T(128)} %constant.105) | copy-start | bytes 388
  373.6 394.0 %all-reduce.15.cloned.1.call-start = ((), (), s32[]{:S(2)}) async-start(), calls=%async_computation.24 | async-start | bytes 4325376 | tf_op jit(solution)/shard_map/psum | solution.py:275
  666.2 19.5 %copy-start.14 = (bf16[256,1024]{1,0:T(8,128)(2,1)S(1)}, bf16[256,1024]{1,0:T(8,128)(2,1)}, u32[]{:S(2)}) copy-start(bf16[256,1024]{1,0:T(8,128)(2,1)} %get-tuple-element.56) | copy-start | bytes 1572868
  (52 other events, 99.7 us)
Sparse Core Ops, SparseCore 0:
  9.6 22.7 all-gather.6
  34.0 22.8 all-gather.8
  71.6 42.1 all-reduce.8
  115.4 50.5 all-gather.10
  167.6 50.5 all-gather.12
  219.7 50.3 all-gather.14
  284.3 28.5 all-reduce.10
  330.8 40.2 all-reduce.12
  373.5 26.2 reduce-scatter.27
  402.0 56.7 reduce-scatter.29
  461.2 25.6 reduce-scatter.19
  489.0 29.0 reduce-scatter.17
  521.1 30.5 reduce-scatter.15
  554.0 56.5 reduce-scatter.21
  612.9 53.2 reduce-scatter.23
  668.9 25.2 reduce-scatter.25
  697.9 69.6 all-reduce.14
where the time goes:
time: 784 us; the launch traced here: 781 us
  waiting for transfers between devices  579 us (74%)
  blocking collectives  70.3 us (9%)
  matrix products  62.5 us (8%)
  other arithmetic  26.6 us (3%)
  local copies, waits for them, and re-layouts  25.9 us (3%)
  between operations  15.5 us (2%)
    unnamed x20, waiting for transfers between devices  94.1 us
    psum x1, waiting for transfers between devices, local(): lax.psum(query_grad.astype(jnp.bfloat16), 'replica').astype(jnp.float32)  66.5 us
    reduce_scatter x1, waiting for transfers between devices, local(): lax.psum_scatter(swiglu_parts[0].astype(jnp.bfloat16), 'fsdp', scatter_di...  58.9 us
    reduce_scatter x1, waiting for transfers between devices, local(): lax.psum_scatter(swiglu_parts[1].astype(jnp.bfloat16), 'fsdp', scatter_di...  55.6 us
    all_gather x1, waiting for transfers between devices, local(): lax.all_gather(gate_weight, 'fsdp', axis=0, tiled=True)  49.6 us
    all_gather x1, waiting for transfers between devices, local(): lax.all_gather(up_weight, 'fsdp', axis=0, tiled=True)  46.9 us
    all_gather x1, waiting for transfers between devices, local(): lax.all_gather(down_weight, 'fsdp', axis=1, tiled=True)  46.6 us
    psum x1, waiting for transfers between devices, local(): attention_total = lax.psum(matmul(mixed_low, out_full), 'tensor')  39 us
  transfers between devices with their start and end apart: 17, of which 15 were waited for; matrix products, arithmetic and copies ran while one was open for 9% of the time, Pallas kernels for 0%

commit v1 on v0

--- a/solution.py
+++ b/solution.py
@@ -1,8 +1,11 @@
+import functools
 import math
 
 import jax
 import jax.numpy as jnp
 from jax import lax
+from jax.experimental import pallas as pl
+from jax.experimental.pallas import tpu as pltpu
 from jax.sharding import PartitionSpec as P
 
 HD = 64
@@ -52,6 +55,358 @@
     return lax.dot_general(
         left, right, (((1,), (1,)), ((), ())), preferred_element_type=jnp.float32
     )
+
+
+MESH = pl.DeviceIdType.MESH
+vmem_bytes = 60 * 1024 * 1024
+
+
+def place():
+    replica = lax.axis_index("replica")
+    index = lax.axis_index("fsdp")
+    return replica, index, index // 2, index % 2
+
+
+def greet(replica, index, line, line_size, core):
+    barrier = pltpu.get_barrier_semaphore()
+    other_core = index + 1 - 2 * core
+    other_replica = replica + 1 - 2 * (replica % 2)
+    pl.semaphore_signal(barrier, inc=1, device_id={"fsdp": other_core}, device_id_type=MESH)
+    pl.semaphore_signal(barrier, inc=1, device_id={"replica": other_replica}, device_id_type=MESH)
+
+    @pl.when(line < line_size - 1)
+    def _():
+        pl.semaphore_signal(barrier, inc=1, device_id={"fsdp": index + 2}, device_id_type=MESH)
+
+    @pl.when(line > 0)
+    def _():
+        pl.semaphore_signal(barrier, inc=1, device_id={"fsdp": index - 2}, device_id_type=MESH)
+
+    ends = (line == 0).astype(jnp.int32) + (line == line_size - 1).astype(jnp.int32)
+    pl.semaphore_wait(barrier, 4 - ends)
+
+
+def remote(source, target, send, receive, where):
+    return pltpu.make_async_remote_copy(
+        src_ref=source,
+        dst_ref=target,
+        send_sem=send,
+        recv_sem=receive,
+        device_id=where,
+        device_id_type=MESH,
+    )
+
+
+def gather_kernel(line_size, pieces, *refs):
+    shards, wholes, sems = refs[:pieces], refs[pieces : 2 * pieces], refs[2 * pieces :]
+    own_sem, core_s, core_r, line_s, line_r, pair_s, pair_r, one_s, one_r, two_s, two_r = sems
+    replica, index, line, core = place()
+    half = replica % 2
+    to_core = {"fsdp": index + 1 - 2 * core}
+    to_pair = {"replica": replica + 1 - 2 * half}
+    neighbours = ({"fsdp": index + 2}, {"fsdp": index - 2})
+    may_send = (line < line_size - 1, line > 0)
+    started = []
+
+    def begin(condition, copy):
+        if condition is None:
+            copy.start()
+        else:
+            pl.when(condition)(copy.start)
+        started.append((condition, copy))
+
+    def slot(position, which_core, which_half):
+        return 4 * position + 2 * which_core + which_half
+
+    greet(replica, index, line, line_size, core)
+    own_copies = []
+    for p in range(pieces):
+        for way in range(2):
+            begin(
+                may_send[way],
+                remote(
+                    shards[p].at[half],
+                    wholes[p].at[slot(line, core, half)],
+                    line_s.at[way, 0, p],
+                    line_r.at[way, 0, p],
+                    neighbours[way],
+                ),
+            )
+    for p in range(pieces):
+        target = wholes[p].at[pl.ds(2 * index, 2)]
+        begin(None, remote(shards[p], target, core_s.at[p], core_r.at[p], to_core))
+        copy = pltpu.make_async_copy(shards[p], target, own_sem.at[p])
+        copy.start()
+        own_copies.append(copy)
+
+    def source_of(way, hop):
+        position = line - hop if way == 0 else line + hop
+        return position, (position >= 0 if way == 0 else position <= line_size - 1)
+
+    def spread(hop):
+        for p in range(pieces):
+            for way in range(2):
+                position, present = source_of(way, hop)
+                place_here = wholes[p].at[slot(position, core, 1 - half)]
+                arrival = remote(
+                    place_here,
+                    place_here,
+                    pair_s.at[way, hop - 1, p],
+                    pair_r.at[way, hop - 1, p],
+                    to_pair,
+                )
+                pl.when(present)(arrival.wait_recv)
+                begin(
+                    present,
+                    remote(
+                        place_here,
+                        place_here,
+                        two_s.at[way, hop - 1, p],
+                        two_r.at[way, hop - 1, p],
+                        to_core,
+                    ),
+                )
+
+    for hop in range(1, line_size):
+        for p in range(pieces):
+            for way in range(2):
+                position, present = source_of(way, hop)
+                block = wholes[p].at[slot(position, core, half)]
+                arrival = remote(
+                    block,
+                    block,
+                    line_s.at[way, hop - 1, p],
+                    line_r.at[way, hop - 1, p],
+                    neighbours[way],
+                )
+                pl.when(present)(arrival.wait_recv)
+                if hop < line_size - 1:
+                    begin(
+                        jnp.logical_and(present, may_send[way]),
+                        remote(
+                            block,
+                            block,
+                            line_s.at[way, hop, p],
+                            line_r.at[way, hop, p],
+                            neighbours[way],
+                        ),
+                    )
+                begin(
+                    present,
+                    remote(
+                        block,
+                        block,
+                        pair_s.at[way, hop - 1, p],
+                        pair_r.at[way, hop - 1, p],
+                        to_pair,
+                    ),
+                )
+                begin(
+                    present,
+                    remote(
+                        block,
+                        block,
+                        one_s.at[way, hop - 1, p],
+                        one_r.at[way, hop - 1, p],
+                        to_core,
+                    ),
+                )
+        if hop > 1:
+            spread(hop - 1)
+    spread(line_size - 1)
+    for p in range(pieces):
+        own_copies[p].wait()
+        target = wholes[p].at[pl.ds(2 * (index + 1 - 2 * core), 2)]
+        remote(target, target, core_s.at[p], core_r.at[p], to_core).wait_recv()
+        for hop in range(1, line_size):
+            for way in range(2):
+                position, present = source_of(way, hop)
+                first = wholes[p].at[slot(position, 1 - core, half)]
+                second = wholes[p].at[slot(position, 1 - core, 1 - half)]
+                sems_at = (way, hop - 1, p)
+                pl.when(present)(
+                    remote(first, first, one_s.at[sems_at], one_r.at[sems_at], to_core).wait_recv
+                )
+                pl.when(present)(
+                    remote(second, second, two_s.at[sems_at], two_r.at[sems_at], to_core).wait_recv
+                )
+    for condition, copy in started:
+        if condition is None:
+            copy.wait_send()
+        else:
+            pl.when(condition)(copy.wait_send)
+
+
+def gather_shards(shards):
+    size = lax.axis_size("fsdp")
+    line_size = size // 2
+    pieces = len(shards)
+    split = [shard.reshape(2, shard.shape[0] // 2, shard.shape[1]) for shard in shards]
+    hops = (2, line_size - 1, pieces)
+    wholes = pl.pallas_call(
+        functools.partial(gather_kernel, line_size, pieces),
+        out_shape=[
+            jax.ShapeDtypeStruct((2 * size,) + shard.shape[1:], shard.dtype) for shard in split
+        ],
+        in_specs=[pl.BlockSpec(memory_space=pl.ANY)] * pieces,
+        out_specs=[pl.BlockSpec(memory_space=pl.ANY)] * pieces,
+        scratch_shapes=[pltpu.SemaphoreType.DMA((pieces,))] * 3
+        + [pltpu.SemaphoreType.DMA(hops)] * 8,
+        compiler_params=pltpu.CompilerParams(
+            collective_id=0, has_side_effects=True, vmem_limit_bytes=vmem_bytes
+        ),
+    )(*split)
+    return [whole.reshape(-1, whole.shape[2]) for whole in wholes]
+
+
+def reduce_kernel(line_size, pieces, *refs):
+    parts, sums = refs[:pieces], refs[pieces : 2 * pieces]
+    core_bufs = refs[2 * pieces : 3 * pieces]
+    pair_bufs = refs[3 * pieces : 4 * pieces]
+    line_bufs = refs[4 * pieces : 5 * pieces]
+    last_bufs = refs[5 * pieces : 6 * pieces]
+    core_s, core_r, pair_s, pair_r, line_s, line_r, last_r, end_s, end_r = refs[6 * pieces :]
+    replica, index, line, core = place()
+    half = replica % 2
+    to_core = {"fsdp": index + 1 - 2 * core}
+    to_pair = {"replica": replica + 1 - 2 * half}
+    right, left = {"fsdp": index + 2}, {"fsdp": index - 2}
+    order = []
+    for step in range((line_size + 1) // 2):
+        order.append(line_size - 1 - step)
+        if step != line_size - 1 - step:
+            order.append(step)
+    started = []
+
+    def begin(condition, copy):
+        if condition is None:
+            copy.start()
+        else:
+            pl.when(condition)(copy.start)
+        started.append((condition, copy))
+
+    greet(replica, index, line, line_size, core)
+    for s in order:
+        for p in range(pieces):
+            begin(
+                None,
+                remote(
+                    parts[p].at[pl.ds(4 * s + 2 * (1 - core), 2)],
+                    core_bufs[p].at[s],
+                    core_s.at[s, p],
+                    core_r.at[s, p],
+                    to_core,
+                ),
+            )
+    for s in order:
+        for p in range(pieces):
+            arrived = core_bufs[p].at[s]
+            remote(arrived, arrived, core_s.at[s, p], core_r.at[s, p], to_core).wait_recv()
+            core_bufs[p][s, 1 - half] = (
+                core_bufs[p][s, 1 - half] + parts[p][4 * s + 2 * core + 1 - half]
+            )
+            begin(
+                None,
+                remote(
+                    core_bufs[p].at[s, 1 - half],
+                    pair_bufs[p].at[s],
+                    pair_s.at[s, p],
+                    pair_r.at[s, p],
+                    to_pair,
+                ),
+            )
+            core_bufs[p][s, half] = core_bufs[p][s, half] + parts[p][4 * s + 2 * core + half]
+    for s in order:
+        for p in range(pieces):
+            arrived = pair_bufs[p].at[s]
+            remote(arrived, arrived, pair_s.at[s, p], pair_r.at[s, p], to_pair).wait_recv()
+            pair_bufs[p][s] = pair_bufs[p][s] + core_bufs[p][s, half]
+            from_line = line_bufs[p].at[s]
+            passes = jnp.logical_or(
+                jnp.logical_and(line < s, line > 0),
+                jnp.logical_and(line > s, line < line_size - 1),
+            )
+
+            @pl.when(passes)
+            def _(s=s, p=p, from_line=from_line):
+                remote(
+                    from_line, from_line, line_s.at[s, p], line_r.at[s, p], right
+                ).wait_recv()
+                pair_bufs[p][s] = pair_bufs[p][s] + line_bufs[p][s]
+
+            begin(
+                line < s,
+                remote(
+                    pair_bufs[p].at[s], from_line, line_s.at[s, p], line_r.at[s, p], right
+                ),
+            )
+            begin(
+                line > s + 1,
+                remote(pair_bufs[p].at[s], from_line, line_s.at[s, p], line_r.at[s, p], left),
+            )
+            begin(
+                line == s + 1,
+                remote(
+                    pair_bufs[p].at[s], last_bufs[p], line_s.at[s, p], last_r.at[p], left
+                ),
+            )
+    for s in order:
+
+        @pl.when(line == s)
+        def _(s=s):
+            for p in range(pieces):
+                if s > 0:
+                    from_line = line_bufs[p].at[s]
+                    remote(
+                        from_line, from_line, line_s.at[s, p], line_r.at[s, p], right
+                    ).wait_recv()
+                    pair_bufs[p][s] = pair_bufs[p][s] + line_bufs[p][s]
+                if s < line_size - 1:
+                    last = last_bufs[p]
+                    remote(last, last, line_s.at[s, p], last_r.at[p], left).wait_recv()
+                    pair_bufs[p][s] = pair_bufs[p][s] + last[...]
+                sums[p][half] = pair_bufs[p][s]
+                remote(
+                    sums[p].at[half], sums[p].at[half], end_s.at[p], end_r.at[p], to_pair
+                ).start()
+
+    for p in range(pieces):
+        remote(
+            sums[p].at[1 - half], sums[p].at[1 - half], end_s.at[p], end_r.at[p], to_pair
+        ).wait_recv()
+        remote(
+            sums[p].at[half], sums[p].at[half], end_s.at[p], end_r.at[p], to_pair
+        ).wait_send()
+    for condition, copy in started:
+        if condition is None:
+            copy.wait_send()
+        else:
+            pl.when(condition)(copy.wait_send)
+
+
+def reduce_parts(parts):
+    size = lax.axis_size("fsdp")
+    line_size = size // 2
+    pieces = len(parts)
+    split = [part.reshape(2 * size, -1, part.shape[1]) for part in parts]
+    blocks = [part.shape[1:] for part in split]
+    kind = jnp.bfloat16
+    sums = pl.pallas_call(
+        functools.partial(reduce_kernel, line_size, pieces),
+        out_shape=[jax.ShapeDtypeStruct((2,) + block, kind) for block in blocks],
+        in_specs=[pl.BlockSpec(memory_space=pltpu.VMEM)] * pieces,
+        out_specs=[pl.BlockSpec(memory_space=pltpu.VMEM)] * pieces,
+        scratch_shapes=[pltpu.VMEM((line_size, 2) + block, kind) for block in blocks]
+        + [pltpu.VMEM((line_size,) + block, kind) for block in blocks]
+        + [pltpu.VMEM((line_size,) + block, kind) for block in blocks]
+        + [pltpu.VMEM(block, kind) for block in blocks]
+        + [pltpu.SemaphoreType.DMA((line_size, pieces))] * 6
+        + [pltpu.SemaphoreType.DMA((pieces,))] * 3,
+        compiler_params=pltpu.CompilerParams(
+            collective_id=1, has_side_effects=True, vmem_limit_bytes=vmem_bytes
+        ),
+    )(*split)
+    return [total.reshape(-1, total.shape[2]) for total in sums]
 
 
 def local(
@@ -68,13 +423,31 @@
     down_weight,
 ):
     length = inputs.shape[0]
-    gains_full, heads_full, query_full, key_full, value_full, out_full = (
-        lax.all_gather(norm_gains, "fsdp", axis=1, tiled=True),
-        lax.all_gather(head_gains, "fsdp", axis=1, tiled=True),
-        lax.all_gather(query_weight, "fsdp", axis=0, tiled=True),
-        lax.all_gather(key_weight, "fsdp", axis=0, tiled=True),
-        lax.all_gather(value_weight, "fsdp", axis=0, tiled=True),
-        lax.all_gather(out_weight, "fsdp", axis=1, tiled=True),
+    devices = lax.axis_size("fsdp")
+    rows = query_weight.shape[0]
+    head_rows = head_gains.shape[1]
+    small = jnp.concatenate(
+        [norm_gains.T, jnp.pad(head_gains.T, ((0, rows - head_rows), (0, 0)))], axis=1
+    )
+    attention_shard = jnp.concatenate(
+        [query_weight, key_weight, value_weight, out_weight.T, jnp.pad(small, ((0, 0), (0, 124)))],
+        axis=1,
+    )
+    attention_full, gate_full, up_full, down_full = gather_shards(
+        [attention_shard, gate_weight, up_weight, down_weight.T]
+    )
+    marks = [query_weight.shape[1], key_weight.shape[1], value_weight.shape[1], out_weight.shape[0]]
+    marks = [sum(marks[: at + 1]) for at in range(4)]
+    query_full = attention_full[:, : marks[0]]
+    key_full = attention_full[:, marks[0] : marks[1]]
+    value_full = attention_full[:, marks[1] : marks[2]]
+    out_full = attention_full[:, marks[2] : marks[3]]
+    gains_full = attention_full[:, marks[3] : marks[3] + 2].T
+    heads_full = (
+        attention_full[:, marks[3] + 2 : marks[3] + 4]
+        .reshape(devices, rows, 2)[:, :head_rows]
+        .reshape(HD, 2)
+        .T
     )
     cosine_table, sine_table = rope_tables(length)
     local_heads = query_full.shape[1] // HD
@@ -121,13 +494,8 @@
         "kgqt,tkd->qkgd", softmax_low, value_low, preferred_element_type=jnp.float32
     )
     mixed_low = mixed_parts.astype(jnp.bfloat16).reshape(length, local_heads * HD)
-    attention_total = lax.psum(matmul(mixed_low, out_full), "tensor")
+    attention_total = lax.psum(cross_cols(mixed_low, out_full), "tensor")
     hidden = residual_in + attention_total
-    gate_full, up_full, down_full = (
-        lax.all_gather(gate_weight, "fsdp", axis=0, tiled=True),
-        lax.all_gather(up_weight, "fsdp", axis=0, tiled=True),
-        lax.all_gather(down_weight, "fsdp", axis=1, tiled=True),
-    )
     second_scale = inverse_rms(hidden)
     second_hat = hidden * second_scale
     second_gain = gains_full[1].astype(jnp.float32)
@@ -137,38 +505,17 @@
     sigmoid_gate = jax.nn.sigmoid(gate_value)
     swish = gate_value * sigmoid_gate
     inner_low = (swish * up_value).astype(jnp.bfloat16)
-    swiglu_total = lax.psum(matmul(inner_low, down_full).astype(jnp.bfloat16), "tensor").astype(
+    swiglu_total = lax.psum(cross_cols(inner_low, down_full).astype(jnp.bfloat16), "tensor").astype(
         jnp.float32
     )
     output = (hidden + swiglu_total).astype(jnp.bfloat16)
-    gate_back, up_back, down_back = (
-        lax.all_gather(gate_weight, "fsdp", axis=0, tiled=True),
-        lax.all_gather(up_weight, "fsdp", axis=0, tiled=True),
-        lax.all_gather(down_weight, "fsdp", axis=1, tiled=True),
-    )
-    grad_inner = cross_cols(cotangent, down_back)
+    grad_inner = matmul(cotangent, down_full)
     grad_gate = (
         grad_inner * up_value * sigmoid_gate * (1.0 + gate_value * (1.0 - sigmoid_gate))
     ).astype(jnp.bfloat16)
     grad_up = (grad_inner * swish).astype(jnp.bfloat16)
-    swiglu_parts = (
-        cross_rows(second_low, grad_gate),
-        cross_rows(second_low, grad_up),
-        cross_rows(inner_low, cotangent),
-    )
-    gate_grad, up_grad, down_grad = (
-        lax.psum_scatter(
-            swiglu_parts[0].astype(jnp.bfloat16), "fsdp", scatter_dimension=0, tiled=True
-        ).astype(jnp.float32),
-        lax.psum_scatter(
-            swiglu_parts[1].astype(jnp.bfloat16), "fsdp", scatter_dimension=0, tiled=True
-        ).astype(jnp.float32),
-        lax.psum_scatter(
-            swiglu_parts[2].astype(jnp.bfloat16), "fsdp", scatter_dimension=1, tiled=True
-        ).astype(jnp.float32),
-    )
     grad_second = lax.psum(
-        (cross_cols(grad_gate, gate_back) + cross_cols(grad_up, up_back)).astype(jnp.bfloat16),
+        (cross_cols(grad_gate, gate_full) + cross_cols(grad_up, up_full)).astype(jnp.bfloat16),
         "tensor",
     ).astype(jnp.float32)
     second_gain_grad = jnp.sum(grad_second * second_hat, axis=0)
@@ -176,17 +523,9 @@
         grad_second, second_hat, second_scale, second_gain
     )
     grad_hidden_low = grad_hidden.astype(jnp.bfloat16)
-    gains_back, heads_back, query_back, key_back, value_back, out_back = (
-        lax.all_gather(norm_gains, "fsdp", axis=1, tiled=True),
-        lax.all_gather(head_gains, "fsdp", axis=1, tiled=True),
-        lax.all_gather(query_weight, "fsdp", axis=0, tiled=True),
-        lax.all_gather(key_weight, "fsdp", axis=0, tiled=True),
-        lax.all_gather(value_weight, "fsdp", axis=0, tiled=True),
-        lax.all_gather(out_weight, "fsdp", axis=1, tiled=True),
-    )
-    out_part = cross_rows(mixed_low, grad_hidden_low)
+    out_part = cross_rows(grad_hidden_low, mixed_low)
     grad_mixed = (
-        cross_cols(grad_hidden_low, out_back)
+        matmul(grad_hidden_low, out_full)
         .astype(jnp.bfloat16)
         .reshape(length, local_groups, group_size, HD)
     )
@@ -234,9 +573,9 @@
     key_part = cross_rows(first_low, grad_key)
     value_part = cross_rows(first_low, grad_value)
     first_part = (
-        cross_cols(grad_query, query_back)
-        + cross_cols(grad_key, key_back)
-        + cross_cols(grad_value, value_back)
+        cross_cols(grad_query, query_full)
+        + cross_cols(grad_key, key_full)
+        + cross_cols(grad_value, value_full)
     )
     grad_first, head_part = (
         lax.psum(first_part.astype(jnp.bfloat16), "tensor").astype(jnp.float32),
@@ -249,49 +588,37 @@
         jnp.bfloat16
     )
     gains_part = jnp.stack([first_gain_grad, second_gain_grad])
-    gains_grad, heads_grad, query_grad, key_grad, value_grad, out_grad = (
-        lax.psum_scatter(
-            gains_part.astype(jnp.bfloat16), "fsdp", scatter_dimension=1, tiled=True
-        ).astype(jnp.float32),
-        lax.psum_scatter(
-            head_part.astype(jnp.bfloat16), "fsdp", scatter_dimension=1, tiled=True
-        ).astype(jnp.float32),
-        lax.psum_scatter(
-            query_part.astype(jnp.bfloat16), "fsdp", scatter_dimension=0, tiled=True
-        ).astype(jnp.float32),
-        lax.psum_scatter(
-            key_part.astype(jnp.bfloat16), "fsdp", scatter_dimension=0, tiled=True
-        ).astype(jnp.float32),
-        lax.psum_scatter(
-            value_part.astype(jnp.bfloat16), "fsdp", scatter_dimension=0, tiled=True
-        ).astype(jnp.float32),
-        lax.psum_scatter(
-            out_part.astype(jnp.bfloat16), "fsdp", scatter_dimension=1, tiled=True
-        ).astype(jnp.float32),
-    )
-    summed = (
-        lax.psum(gains_grad.astype(jnp.bfloat16), "replica").astype(jnp.float32),
-        lax.psum(heads_grad.astype(jnp.bfloat16), "replica").astype(jnp.float32),
-        lax.psum(query_grad.astype(jnp.bfloat16), "replica").astype(jnp.float32),
-        lax.psum(key_grad.astype(jnp.bfloat16), "replica").astype(jnp.float32),
-        lax.psum(value_grad.astype(jnp.bfloat16), "replica").astype(jnp.float32),
-        lax.psum(out_grad.astype(jnp.bfloat16), "replica").astype(jnp.float32),
-        lax.psum(gate_grad.astype(jnp.bfloat16), "replica").astype(jnp.float32),
-        lax.psum(up_grad.astype(jnp.bfloat16), "replica").astype(jnp.float32),
-        lax.psum(down_grad.astype(jnp.bfloat16), "replica").astype(jnp.float32),
-    )
+    heads_part = jnp.pad(
+        head_part.T.reshape(devices, head_rows, 2), ((0, 0), (0, rows - head_rows), (0, 0))
+    ).reshape(devices * rows, 2)
+    small_part = jnp.pad(jnp.concatenate([gains_part.T, heads_part], axis=1), ((0, 0), (0, 124)))
+    attention_part = jnp.concatenate(
+        [query_part, key_part, value_part, out_part, small_part], axis=1
+    ).astype(jnp.bfloat16)
+    summed = reduce_parts(
+        [
+            cross_rows(second_low, grad_gate).astype(jnp.bfloat16),
+            cross_rows(second_low, grad_up).astype(jnp.bfloat16),
+            cross_rows(cotangent, inner_low).astype(jnp.bfloat16),
+            attention_part,
+        ]
+    )
+    replicas = lax.axis_size("replica")
+    if replicas > 2:
+        summed = [lax.psum(total, "replica") * 0.5 for total in summed]
+    gate_grad, up_grad, down_grad, attention_grad = [total.astype(jnp.float32) for total in summed]
     return (
         output,
         input_grad,
-        summed[0],
-        summed[1],
-        summed[2],
-        summed[3],
-        summed[4],
-        summed[5],
-        summed[6],
-        summed[7],
-        summed[8],
+        attention_grad[:, marks[3] : marks[3] + 2].T,
+        attention_grad[:head_rows, marks[3] + 2 : marks[3] + 4].T,
+        attention_grad[:, : marks[0]],
+        attention_grad[:, marks[0] : marks[1]],
+        attention_grad[:, marks[1] : marks[2]],
+        attention_grad[:, marks[2] : marks[3]].T,
+        gate_grad,
+        up_grad,
+        down_grad.T,
     )
 
 

time: 784 us -> 434 us (0.55)
  waiting for transfers between devices: 579 us -> 83.2 us
  Pallas kernels: 0 us -> 225 us
  blocking collectives: 70.3 us -> 4.98 us
  matrix products: 62.5 us -> 52.8 us
    pallas_call x0 -> x2, Pallas kernels: none -> 225 us  [the longest x1 142 us: reduce_parts(): pl.pallas_call(functools.partial(reduce_kernel, line_size, pieces), out_s...]
    reduce_scatter x5 -> x0, waiting for transfers between devices: 205 us -> none  [the longest x1 58.9 us: local(): lax.psum_scatter(swiglu_parts[0].astype(jnp.bfloat16), 'fsdp', scatter_di...]
    all_gather x5 -> x0, waiting for transfers between devices: 143 us -> none  [the longest x1 49.6 us: local(): lax.all_gather(gate_weight, 'fsdp', axis=0, tiled=True)]
    unnamed x20 -> x3, waiting for transfers between devices: 94.1 us -> 0.05 us
    psum x4 -> x3, waiting for transfers between devices: 137 us -> 83.1 us  [the longest x1 39.5 us: local(): attention_total = lax.psum(cross_cols(mixed_low, out_full), 'tensor')]
    all_gather x4 -> x0, blocking collectives: 49.5 us -> none  [the longest x1 16.3 us: local(): lax.all_gather(key_weight, 'fsdp', axis=0, tiled=True)]
    unnamed x1 -> x0, blocking collectives: 11 us -> none
    unnamed x143 -> x132, local copies, waits for them, and re-layouts: 19 us -> 11.2 us
  transfers between devices with their start and end apart: 17 -> 3, of which waited for: 15 -> 3; matrix products, arithmetic and copies ran while one was open for 9% -> 5% of each run, Pallas kernels for 0% -> 0%
where the time goes in v1:
time: 434 us; the launch traced here: 433 us
  Pallas kernels  225 us (52%)
  waiting for transfers between devices  83.2 us (19%)
  matrix products  52.8 us (12%)
  local copies, waits for them, and re-layouts  28.5 us (7%)
  other arithmetic  22.7 us (5%)
  between operations  14.8 us (3%)
  blocking collectives  4.98 us (1%)
    pallas_call x1, Pallas kernels, reduce_parts(): pl.pallas_call(functools.partial(reduce_kernel, line_size, pieces), out_s...  142 us
    pallas_call x1, Pallas kernels, gather_shards(): pl.pallas_call(functools.partial(gather_kernel, line_size, pieces), out_s...  82.9 us
    psum x1, waiting for transfers between devices, local(): attention_total = lax.psum(cross_cols(mixed_low, out_full), 'tensor')  39.5 us
    psum x1, waiting for transfers between devices, local(): lax.psum(cross_cols(inner_low, down_full).astype(jnp.bfloat16), 'tensor')  24.8 us
    psum x1, waiting for transfers between devices, local(): lax.psum((cross_cols(grad_gate, gate_full) + cross_cols(grad_up, up_full)...  18.7 us
    dot_general x7, matrix products, cross_rows(): lax.dot_general(left, right, (((0,), (0,)), ((), ())), preferred_element_...  17.1 us
    dot_general x7, matrix products, cross_cols(): lax.dot_general(left, right, (((1,), (1,)), ((), ())), preferred_element_...  16.4 us
    dot_general x7, matrix products, matmul(): return jnp.dot(left, right, preferred_element_type=jnp.float32)  15.6 us
  transfers between devices with their start and end apart: 3, of which 3 were waited for; matrix products, arithmetic and copies ran while one was open for 5% of the time, Pallas kernels for 0%

profile of v1, /device:TPU:16, one launch (start us, length us, event | category | flops | bytes accessed | tf_op | source)
XLA Modules:
  0.0 432.7 jit_solution(131845818514693447)
XLA Ops:
  14.0 82.9 %shard_map.204 = (bf16[16,64,1664]{2,1,0:T(8,128)(2,1)}, bf16[16,64,2304]{2,1,0:T(8,128)(2,1)}, bf16[16,64,2304]{2,1,0:T(8,128)(2,1)}, bf16[16,64,2304]{2,1,0:T(8,128)(2,1)}) custom-call(bf16[2,64,1664]{2,1,0:T(8,128)(2,1)} %bitcast.224, bf16[2,64,2304]{2,1,0:T(8,128)(2,1)} %bitcast.233, bf16[2,64,2304]{2,1,0:T(8,128)(2,1)} %bitcast.234, ...), custom_call_target="tpu_custom_call" | custom-call | tf_op jit(solution)/shard_map/pallas_call | solution.py:246
  98.4 1.7 fusion.38
  100.2 1.7 multiply_reduce_fusion.5
  101.9 1.5 convolution_convert_fusion.10
  106.7 2.8 fusion.34
  112.1 39.5 %all-reduce.9.cloned.1.call-done = f32[256,1024]{1,0:T(8,128)} async-done(((f32[256,1024]{1,0:T(8,128)}), f32[256,1024]{1,0:T(8,128)}) %all-reduce.9.cloned.1.call-update) | async-done | bytes 1048592 | tf_op jit(solution)/shard_map/psum | solution.py:497
  151.7 1.6 multiply_reduce_fusion
  153.5 4.0 fusion.69
  159.0 2.9 multiply_convert_fusion
  163.3 3.6 convolution_convert_fusion.1
  166.9 2.2 fusion.12
  169.4 5.1 %convolution_convert_fusion.2 = bf16[1024,2304]{1,0:T(8,128)(2,1)} fusion(bf16[256,1024]{1,0:T(8,128)(2,1)} %copy-done.4, bf16[256,2304]{1,0:T(8,128)(2,1)} %copy-done.17), kind=kOutput, calls=%fused_computation.2 | convolution fusion | flops 1210318848 | bytes 6422528 | tf_op jit(solution)/shard_map/dot_general | solution.py:49
  174.6 4.6 %convolution_convert_fusion.7 = bf16[256,1024]{1,0:T(8,128)(2,1)} fusion(bf16[256,2304]{1,0:T(8,128)(2,1)S(1)} %copy-done.7, bf16[1024,2304]{1,0:T(8,128)(2,1)} %bitcast.266), kind=kOutput, calls=%fused_computation.38 | convolution fusion | flops 1208221696 | bytes 6422528 | tf_op jit(solution)/shard_map/dot_general | solution.py:55
  179.2 18.7 %all-reduce.11.cloned.1.call-done = bf16[256,1024]{1,0:T(8,128)(2,1)} async-done(((bf16[256,1024]{1,0:T(8,128)(2,1)}), bf16[256,1024]{1,0:T(8,128)(2,1)}) %all-reduce.11.cloned.1.call-update) | async-done | bytes 524304 | tf_op jit(solution)/shard_map/psum | solution.py:517
  197.9 2.1 fusion.26
  200.0 2.3 convert_bitcast_fusion
  203.3 2.4 convolution_convert_fusion.8
  213.6 1.9 multiply_reduce_fusion.1
  215.4 1.8 fusion.36
  218.0 1.5 convolution_add_fusion.1
  219.5 2.2 fusion.13
  221.8 3.7 convolution_convert_fusion
  227.1 5.0 %psum.39 = bf16[8,8,2]{1,0,2:T(8,128)(2,1)S(1)} all-reduce(bf16[8,8,2]{1,0,2:T(8,128)(2,1)S(1)} %reshape.350), channel_id=1, replica_groups=mesh['replica'=2,'fsdp'=8,'tensor'=2] {'tensor'}, use_global_device_ids=true, to_apply=%region_21.22 | all-reduce | flops 128 | bytes 512 | tf_op jit(solution)/shard_map/psum | solution.py:582
  233.4 1.5 convolution_convert_fusion.4
  237.4 24.8 %all-reduce.13.cloned.1.call-done = (bf16[256,1024]{1,0:T(8,128)(2,1)}, bf16[256,1024]{1,0:T(8,128)(2,1)}) async-done(((bf16[256,1024]{1,0:T(8,128)(2,1)}, bf16[256,1024]{1,0:T(8,128)(2,1)}), (bf16[256,1024]{1,0:T(8,128)(2,1)}, bf16[256,1024]{1,0:T(8,128)(2,1)})) %all-reduce.13.cloned.1.call-update) | async-done | bytes 1048592 | tf_op jit(solution)/shard_map/psum | solution.py:508
  262.2 2.1 fusion.29
  267.7 1.5 fusion.10
  270.0 142.4 %shard_map.205 = (bf16[2,64,2304]{2,1,0:T(8,128)(2,1)}, bf16[2,64,2304]{2,1,0:T(8,128)(2,1)}, bf16[2,64,2304]{2,1,0:T(8,128)(2,1)}, bf16[2,64,1664]{2,1,0:T(8,128)(2,1)}) custom-call(bf16[16,64,2304]{2,1,0:T(8,128)(2,1)} %bitcast.204, bf16[16,64,2304]{2,1,0:T(8,128)(2,1)} %bitcast.203, bf16[16,64,2304]{2,1,0:T(8,128)(2,1)} %bitcast.205, ...), custom_call_target="tpu_custom_call" | custom-call | tf_op jit(solution)/shard_map/pallas_call | solution.py:394
  415.1 1.6 bitcast_convert_fusion
  416.8 2.8 copy.104
  420.4 2.2 bitcast_convert_fusion.2
  423.8 2.3 fusion.22
  (216 shorter events, 41.0 us)
Async XLA Ops:
  7.2 5.7 %copy-start.26 = (bf16[2304,128]{1,0:T(8,128)(2,1)S(1)}, bf16[2304,128]{1,0:T(8,128)(2,1)}, u32[]{:S(2)}) copy-start(bf16[2304,128]{1,0:T(8,128)(2,1)} %param.29) | copy-start | bytes 1769476
  7.2 144.5 %all-reduce.9.cloned.1.call-start = ((), (), s32[]{:S(2)}) async-start(), calls=%async_computation | async-start | bytes 2097152 | tf_op jit(solution)/shard_map/psum | solution.py:497
  12.9 85.3 %copy-start.2 = (bf16[256,1024]{1,0:T(8,128)(2,1)S(1)}, bf16[256,1024]{1,0:T(8,128)(2,1)}, u32[]{:S(2)}) copy-start(bf16[256,1024]{1,0:T(8,128)(2,1)} %param.19) | copy-start | bytes 1572868
  98.2 3.7 copy-start.39
  98.4 5.0 %copy-start.42 = (f32[256]{0:T(256)}, f32[256]{0:T(256)S(1)}, u32[]{:S(2)}) copy-start(f32[256]{0:T(256)S(1)} %add_rsqrt_fusion.3) | copy-start | bytes 3076
  100.2 3.6 copy-start.14
  101.9 3.1 copy-start.9
  103.9 5.9 %copy-start.48 = (f32[64]{0:T(128)}, f32[64]{0:T(128)S(1)}, u32[]{:S(2)}) copy-start(f32[64]{0:T(128)S(1)} %get-tuple-element.141) | copy-start | bytes 772
  103.9 7.6 %copy-start.46 = (f32[64]{0:T(128)}, f32[64]{0:T(128)S(1)}, u32[]{:S(2)}) copy-start(f32[64]{0:T(128)S(1)} %get-tuple-element.142) | copy-start | bytes 772
  109.5 88.4 %all-reduce.11.cloned.1.call-start = ((), (), s32[]{:S(2)}) async-start(), calls=%async_computation.1 | async-start | bytes 1048576 | tf_op jit(solution)/shard_map/psum | solution.py:517
  153.3 4.2 slice-start.4
  153.5 9.8 %copy-start.4 = (bf16[256,1024]{1,0:T(8,128)(2,1)}, bf16[256,1024]{1,0:T(8,128)(2,1)S(1)}, u32[]{:S(2)}) copy-start(bf16[256,1024]{1,0:T(8,128)(2,1)S(1)} %multiply_convert_fusion.3) | copy-start | bytes 1572868
  153.5 4.1 slice-start.5
  153.5 5.5 %slice-start = ((s8[4718592]{0:T(1024)(128)(4,1)}), s8[4194304]{0:T(1024)(128)(4,1)S(1)}, s32[]{:S(2)}) async-start(s8[4718592]{0:T(1024)(128)(4,1)} %bitcast.267), calls=%async_computation.3 | async-start | bytes 8388608
  161.9 5.0 %slice-start.2 = ((s8[4718592]{0:T(1024)(128)(4,1)}), s8[4194304]{0:T(1024)(128)(4,1)S(1)}, s32[]{:S(2)}) async-start(s8[4718592]{0:T(1024)(128)(4,1)} %bitcast.271), calls=%async_computation.5 | async-start | bytes 8388608
  163.3 3.6 slice-start.3
  169.2 93.1 %all-reduce.13.cloned.1.call-start = ((), (), s32[]{:S(2)}) async-start(), calls=%async_computation.2 | async-start | bytes 2097152 | tf_op jit(solution)/shard_map/psum | solution.py:508
  169.4 5.2 %copy-start.7 = (bf16[256,2304]{1,0:T(8,128)(2,1)S(1)}, bf16[256,2304]{1,0:T(8,128)(2,1)}, u32[]{:S(2)}) copy-start(bf16[256,2304]{1,0:T(8,128)(2,1)} %get-tuple-element.112) | copy-start | bytes 3538948
  213.5 3.7 copy-start.21
  213.6 3.7 copy-start.41
  213.6 3.7 copy-start.50
  215.4 4.1 copy-start.20
  218.0 3.8 copy-start.8
  218.0 3.8 copy-start.13
  221.8 3.7 copy-start.45
  221.8 11.6 %copy-start.3 = (bf16[256,1024]{1,0:T(8,128)(2,1)S(1)}, bf16[256,1024]{1,0:T(8,128)(2,1)}, u32[]{:S(2)}) copy-start(bf16[256,1024]{1,0:T(8,128)(2,1)} %param.19) | copy-start | bytes 1572868
  221.8 11.6 %copy-start.40 = (f32[1,1024]{1,0:T(1,128)S(1)}, f32[1,1024]{1,0:T(1,128)}, u32[]{:S(2)}) copy-start(f32[1,1024]{1,0:T(1,128)} %copy-done.39) | copy-start | bytes 12292
  221.8 11.6 %copy-start.43 = (f32[256]{0:T(256)S(1)}, f32[256]{0:T(256)}, u32[]{:S(2)}) copy-start(f32[256]{0:T(256)} %copy-done.42) | copy-start | bytes 3076
  237.4 30.3 %copy-start.19 = (bf16[4,64,2,256]{3,1,2,0:T(8,128)(2,1)S(1)}, bf16[4,64,2,256]{3,1,2,0:T(8,128)(2,1)}, u32[]{:S(2)}) copy-start(bf16[4,64,2,256]{3,1,2,0:T(8,128)(2,1)} %copy-done.18) | copy-start | bytes 786436
  416.8 7.0 %copy-start.51 = (f32[256]{0:T(256)S(1)}, f32[256]{0:T(256)}, u32[]{:S(2)}) copy-start(f32[256]{0:T(256)} %get-tuple-element.103) | copy-start | bytes 3076
  416.8 7.0 %copy-start.1 = (f32[256,1024]{1,0:T(8,128)S(1)}, f32[256,1024]{1,0:T(8,128)}, u32[]{:S(2)}) copy-start(f32[256,1024]{1,0:T(8,128)} %copy-done) | copy-start | bytes 3145732
  416.8 7.0 %copy-start.11 = (bf16[256,1024]{1,0:T(8,128)(2,1)S(1)}, bf16[256,1024]{1,0:T(8,128)(2,1)}, u32[]{:S(2)}) copy-start(bf16[256,1024]{1,0:T(8,128)(2,1)} %get-tuple-element.105) | copy-start | bytes 1572868
  (29 other events, 42.2 us)
Sparse Core Ops, SparseCore 0:
  109.6 42.0 all-reduce.8
  169.3 28.5 all-reduce.10
  221.9 40.3 all-reduce.12

commit v2 on v1

--- a/solution.py
+++ b/solution.py
@@ -95,6 +95,18 @@
         device_id=where,
         device_id_type=MESH,
     )
+
+
+def pair_permute(values, axis):
+    return lax.ppermute(values, axis, [(at, at ^ 1) for at in range(lax.axis_size(axis))])
+
+
+def tensor_sum(values):
+    low = values.astype(jnp.bfloat16)
+    if lax.axis_size("tensor") != 2:
+        return lax.psum(low.astype(jnp.float32), "tensor")
+    other = pair_permute(low, "tensor")
+    return low.astype(jnp.float32) + other.astype(jnp.float32)
 
 
 def gather_kernel(line_size, pieces, *refs):
@@ -494,7 +506,7 @@
         "kgqt,tkd->qkgd", softmax_low, value_low, preferred_element_type=jnp.float32
     )
     mixed_low = mixed_parts.astype(jnp.bfloat16).reshape(length, local_heads * HD)
-    attention_total = lax.psum(cross_cols(mixed_low, out_full), "tensor")
+    attention_total = tensor_sum(cross_cols(mixed_low, out_full))
     hidden = residual_in + attention_total
     second_scale = inverse_rms(hidden)
     second_hat = hidden * second_scale
@@ -505,19 +517,14 @@
     sigmoid_gate = jax.nn.sigmoid(gate_value)
     swish = gate_value * sigmoid_gate
     inner_low = (swish * up_value).astype(jnp.bfloat16)
-    swiglu_total = lax.psum(cross_cols(inner_low, down_full).astype(jnp.bfloat16), "tensor").astype(
-        jnp.float32
-    )
+    swiglu_total = tensor_sum(cross_cols(inner_low, down_full))
     output = (hidden + swiglu_total).astype(jnp.bfloat16)
     grad_inner = matmul(cotangent, down_full)
     grad_gate = (
         grad_inner * up_value * sigmoid_gate * (1.0 + gate_value * (1.0 - sigmoid_gate))
     ).astype(jnp.bfloat16)
     grad_up = (grad_inner * swish).astype(jnp.bfloat16)
-    grad_second = lax.psum(
-        (cross_cols(grad_gate, gate_full) + cross_cols(grad_up, up_full)).astype(jnp.bfloat16),
-        "tensor",
-    ).astype(jnp.float32)
+    grad_second = tensor_sum(cross_cols(grad_gate, gate_full) + cross_cols(grad_up, up_full))
     second_gain_grad = jnp.sum(grad_second * second_hat, axis=0)
     grad_hidden = cotangent.astype(jnp.float32) + norm_back(
         grad_second, second_hat, second_scale, second_gain
@@ -577,12 +584,8 @@
         + cross_cols(grad_key, key_full)
         + cross_cols(grad_value, value_full)
     )
-    grad_first, head_part = (
-        lax.psum(first_part.astype(jnp.bfloat16), "tensor").astype(jnp.float32),
-        lax.psum(jnp.stack([query_gain_grad, key_gain_grad]).astype(jnp.bfloat16), "tensor").astype(
-            jnp.float32
-        ),
-    )
+    grad_first = tensor_sum(first_part)
+    head_part = tensor_sum(jnp.stack([query_gain_grad, key_gain_grad]))
     first_gain_grad = jnp.sum(grad_first * first_hat, axis=0)
     input_grad = (grad_hidden + norm_back(grad_first, first_hat, first_scale, first_gain)).astype(
         jnp.bfloat16

time: 434 us -> 353 us (0.81)
  waiting for transfers between devices: 83.2 us -> 26.7 us
  between operations: 14.8 us -> 1.66 us
  starting transfers between devices: 0.52 us -> 5.76 us
  other arithmetic: 22.7 us -> 17.5 us
  blocking collectives: 4.98 us -> 0 us
    psum x3 -> x0, waiting for transfers between devices: 83.1 us -> none  [the longest x1 39.5 us: local(): attention_total = lax.psum(cross_cols(mixed_low, out_full), 'tensor')]
    ppermute x0 -> x5, waiting for transfers between devices: none -> 26.7 us  [pair_permute(): lax.ppermute(values, axis, [(at, at ^ 1) for at in range(lax.axis_size(ax...]
    ppermute x0 -> x5, starting transfers between devices: none -> 5.76 us  [pair_permute(): lax.ppermute(values, axis, [(at, at ^ 1) for at in range(lax.axis_size(ax...]
    dot_general x7, matrix products: 16.4 us -> 11.4 us  [cross_cols(): lax.dot_general(left, right, (((1,), (1,)), ((), ())), preferred_element_...]
    psum x1 -> x0, blocking collectives: 4.98 us -> none  [local(): lax.psum(jnp.stack([query_gain_grad, key_gain_grad]).astype(jnp.bfloat16)...]
    unnamed x132 -> x118, local copies, waits for them, and re-layouts: 11.2 us -> 11.5 us
  transfers between devices with their start and end apart: 3 -> 5, of which waited for: 3 -> 4; matrix products, arithmetic and copies ran while one was open for 5% -> 6% of each run, Pallas kernels for 0% -> 0%
where the time goes in v2:
time: 353 us; the launch traced here: 352 us
  Pallas kernels  225 us (64%)
  matrix products  49.2 us (14%)
  waiting for transfers between devices  26.7 us (8%)
  local copies, waits for them, and re-layouts  25.9 us (7%)
  other arithmetic  17.5 us (5%)
  starting transfers between devices  5.76 us (2%)
    pallas_call x1, Pallas kernels, reduce_parts(): pl.pallas_call(functools.partial(reduce_kernel, line_size, pieces), out_s...  142 us
    pallas_call x1, Pallas kernels, gather_shards(): pl.pallas_call(functools.partial(gather_kernel, line_size, pieces), out_s...  82.9 us
    ppermute x5, waiting for transfers between devices, pair_permute(): lax.ppermute(values, axis, [(at, at ^ 1) for at in range(lax.axis_size(ax...  26.7 us
    dot_general x7, matrix products, matmul(): return jnp.dot(left, right, preferred_element_type=jnp.float32)  17 us
    dot_general x7, matrix products, cross_rows(): lax.dot_general(left, right, (((0,), (0,)), ((), ())), preferred_element_...  16.5 us
    unnamed x118, local copies, waits for them, and re-layouts  11.5 us
    dot_general x7, matrix products, cross_cols(): lax.dot_general(left, right, (((1,), (1,)), ((), ())), preferred_element_...  11.4 us
  transfers between devices with their start and end apart: 5, of which 4 were waited for; matrix products, arithmetic and copies ran while one was open for 6% of the time, Pallas kernels for 0%

profile of v2, /device:TPU:16, one launch (start us, length us, event | category | flops | bytes accessed | tf_op | source)
XLA Modules:
  0.0 351.9 jit_solution(11183482875899941548)
XLA Ops:
  7.4 82.9 %shard_map.204 = (bf16[16,64,1664]{2,1,0:T(8,128)(2,1)}, bf16[16,64,2304]{2,1,0:T(8,128)(2,1)}, bf16[16,64,2304]{2,1,0:T(8,128)(2,1)}, bf16[16,64,2304]{2,1,0:T(8,128)(2,1)}) custom-call(bf16[2,64,1664]{2,1,0:T(8,128)(2,1)} %bitcast.224, bf16[2,64,2304]{2,1,0:T(8,128)(2,1)} %bitcast.231, bf16[2,64,2304]{2,1,0:T(8,128)(2,1)} %bitcast.232, ...), custom_call_target="tpu_custom_call" | custom-call | tf_op jit(solution)/shard_map/pallas_call | solution.py:258
  91.9 1.7 fusion.33
  93.6 1.7 multiply_reduce_fusion.7
  95.3 1.5 convolution_convert_fusion.11
  101.1 2.5 convolution_convert_fusion.8
  103.6 1.5 collective-permute-start
  106.6 2.0 copy.94
  109.2 3.7 %convolution_bitcast_fusion = f32[256,2304]{1,0:T(8,128)S(1)} fusion(bf16[256,1024]{1,0:T(8,128)(2,1)S(1)} %copy-done.8, bf16[1024,2304]{1,0:T(8,128)(2,1)} %bitcast.276), kind=kOutput, calls=%fused_computation.3 | convolution fusion | flops 1207959552 | bytes 7602176 | tf_op jit(solution)/shard_map/dot_general | solution.py:45
  113.0 5.2 %collective-permute-done = bf16[256,1024]{1,0:T(8,128)(2,1)} collective-permute-done((bf16[256,1024]{1,0:T(8,128)(2,1)}, bf16[256,1024]{1,0:T(8,128)(2,1)}, u32[]{:S(2)}, u32[]{:S(2)}) %collective-permute-start) | collective-permute-done | bytes 524320 | tf_op jit(solution)/shard_map/ppermute | solution.py:101
  118.2 1.5 multiply_reduce_fusion.2
  119.9 3.9 %fusion.63 = f32[256,2304]{1,0:T(8,128)S(1)} fusion(bf16[256,1024]{1,0:T(8,128)(2,1)S(1)} %multiply_convert_fusion.3, bf16[1024,2304]{1,0:T(8,128)(2,1)} %bitcast.268), kind=kOutput, calls=%fused_computation.163 | convolution fusion | flops 1207959552 | bytes 7602176 | tf_op jit(solution)/shard_map/dot_general | solution.py:45
  123.8 2.1 multiply_convert_fusion
  127.4 1.5 fusion.64
  128.9 3.6 %convolution_convert_fusion.1 = bf16[1024,2304]{1,0:T(8,128)(2,1)} fusion(bf16[256,1024]{1,0:T(8,128)(2,1)S(1)} %multiply_convert_fusion.3, bf16[256,2304]{1,0:T(8,128)(2,1)S(1)} %get-tuple-element.108), kind=kOutput, calls=%fused_computation.1 | convolution fusion | flops 1210318848 | bytes 6422528 | tf_op jit(solution)/shard_map/dot_general | solution.py:49
  134.0 1.6 collective-permute-start.2
  135.5 3.6 %convolution_convert_fusion.2 = bf16[1024,2304]{1,0:T(8,128)(2,1)} fusion(bf16[256,1024]{1,0:T(8,128)(2,1)S(1)} %multiply_convert_fusion.3, bf16[256,2304]{1,0:T(8,128)(2,1)S(1)} %get-tuple-element.109), kind=kOutput, calls=%fused_computation.2 | convolution fusion | flops 1210318848 | bytes 6422528 | tf_op jit(solution)/shard_map/dot_general | solution.py:49
  139.7 3.7 %convolution_convert_fusion = bf16[2304,1024]{0,1:T(8,128)(2,1)} fusion(bf16[256,2304]{1,0:T(8,128)(2,1)S(1)} %get-tuple-element.110, bf16[256,1024]{1,0:T(8,128)(2,1)S(1)} %copy-done.8), kind=kOutput, calls=%fused_computation | convolution fusion | flops 1210318848 | bytes 6422528 | tf_op jit(solution)/shard_map/dot_general | solution.py:49
  143.4 5.5 %collective-permute-done.2 = bf16[256,1024]{1,0:T(8,128)(2,1)S(1)} collective-permute-done((bf16[256,1024]{1,0:T(8,128)(2,1)S(1)}, bf16[256,1024]{1,0:T(8,128)(2,1)S(1)}, u32[]{:S(2)}, u32[]{:S(2)}) %collective-permute-start.2) | collective-permute-done | bytes 524320 | tf_op jit(solution)/shard_map/ppermute | solution.py:101
  149.8 9.0 %collective-permute-done.1 = bf16[256,1024]{1,0:T(8,128)(2,1)S(1)} collective-permute-done((bf16[256,1024]{1,0:T(8,128)(2,1)S(1)}, bf16[256,1024]{1,0:T(8,128)(2,1)S(1)}, u32[]{:S(2)}, u32[]{:S(2)}) %collective-permute-start.1) | collective-permute-done | bytes 524320 | tf_op jit(solution)/shard_map/ppermute | solution.py:101
  158.8 1.5 convert_bitcast_fusion
  160.3 2.4 convolution_convert_fusion.9
  171.1 1.7 fusion.31
  172.9 1.5 convolution_convert_fusion.4
  176.7 1.4 fusion.13
  178.1 1.6 collective-permute-start.3
  180.5 2.4 constant_dynamic-update-slice_fusion.5
  184.0 7.0 %collective-permute-done.4 = bf16[2,64]{1,0:T(2,128)(2,1)S(1)} collective-permute-done((bf16[2,64]{1,0:T(2,128)(2,1)S(1)}, bf16[2,64]{1,0:T(2,128)(2,1)S(1)}, u32[]{:S(2)}, u32[]{:S(2)}) %collective-permute-start.4) | collective-permute-done | bytes 288 | tf_op jit(solution)/shard_map/ppermute | solution.py:101
  191.1 1.8 fusion.23
  194.6 2.4 fusion.10
  197.8 142.2 %shard_map.205 = (bf16[2,64,2304]{2,1,0:T(8,128)(2,1)}, bf16[2,64,2304]{2,1,0:T(8,128)(2,1)}, bf16[2,64,2304]{2,1,0:T(8,128)(2,1)}, bf16[2,64,1664]{2,1,0:T(8,128)(2,1)}) custom-call(bf16[16,64,2304]{2,1,0:T(8,128)(2,1)} %bitcast.204, bf16[16,64,2304]{2,1,0:T(8,128)(2,1)} %bitcast.203, bf16[16,64,2304]{2,1,0:T(8,128)(2,1)} %bitcast.205, ...), custom_call_target="tpu_custom_call" | custom-call | tf_op jit(solution)/shard_map/pallas_call | solution.py:406
  346.2 2.2 bitcast_convert_fusion.2
  349.7 2.2 fusion.22
  (203 shorter events, 41.0 us)
Async XLA Ops:
  0.6 5.7 %copy-start.20 = (bf16[2304,128]{1,0:T(8,128)(2,1)S(1)}, bf16[2304,128]{1,0:T(8,128)(2,1)}, u32[]{:S(2)}) copy-start(bf16[2304,128]{1,0:T(8,128)(2,1)} %param.29) | copy-start | bytes 1769476
  6.3 85.3 %copy-start = (bf16[256,1024]{1,0:T(8,128)(2,1)S(1)}, bf16[256,1024]{1,0:T(8,128)(2,1)}, u32[]{:S(2)}) copy-start(bf16[256,1024]{1,0:T(8,128)(2,1)} %param.19) | copy-start | bytes 1572868
  91.7 3.7 %copy-start.35 = (f32[1,1024]{1,0:T(1,128)}, f32[1,1024]{1,0:T(1,128)S(1)}, u32[]{:S(2)}) copy-start(f32[1,1024]{1,0:T(1,128)S(1)} %get-tuple-element.136) | copy-start | bytes 12292
  91.9 3.5 copy-start.37
  93.6 3.6 %copy-start.11 = (f32[256,512]{1,0:T(8,128)}, f32[256,512]{1,0:T(8,128)S(1)}, u32[]{:S(2)}) copy-start(f32[256,512]{1,0:T(8,128)S(1)} %fusion.33) | copy-start | bytes 1572868
  97.3 7.8 %copy-start.41 = (f32[64]{0:T(128)}, f32[64]{0:T(128)S(1)}, u32[]{:S(2)}) copy-start(f32[64]{0:T(128)S(1)} %get-tuple-element.140) | copy-start | bytes 772
  97.3 11.3 %copy-start.39 = (f32[64]{0:T(128)}, f32[64]{0:T(128)S(1)}, u32[]{:S(2)}) copy-start(f32[64]{0:T(128)S(1)} %get-tuple-element.141) | copy-start | bytes 772
  100.4 8.9 %copy-start.8 = (bf16[256,1024]{1,0:T(8,128)(2,1)S(1)}, bf16[256,1024]{1,0:T(8,128)(2,1)}, u32[]{:S(2)}) copy-start(bf16[256,1024]{1,0:T(8,128)(2,1)} %param.20) | copy-start | bytes 1572868
  103.6 14.6 %collective-permute-start = (bf16[256,1024]{1,0:T(8,128)(2,1)}, bf16[256,1024]{1,0:T(8,128)(2,1)}, u32[]{:S(2)}, u32[]{:S(2)}) collective-permute-start(bf16[256,1024]{1,0:T(8,128)(2,1)} %convolution_convert_fusion.8), channel_id=1, source_target_pairs={{0,1},{1,0},{2,3},{3,2},{4,5},{5,4},{6,7},{7,6},{8,9},{9,8},{10,11... | collective-permute-start | bytes 1572872 | tf_op jit(solution)/shard_map/ppermute | solution.py:101
  119.7 4.1 %slice-start.2 = ((s8[4718592]{0:T(1024)(128)(4,1)}), s8[4194304]{0:T(1024)(128)(4,1)S(1)}, s32[]{:S(2)}) async-start(s8[4718592]{0:T(1024)(128)(4,1)} %bitcast.272), calls=%async_computation.2 | async-start | bytes 8388608
  119.9 3.9 %slice-start.3 = ((s8[4718592]{0:T(1024)(128)(4,1)}), s8[524288]{0:T(1024)(128)(4,1)S(1)}, s32[]{:S(2)}) async-start(s8[4718592]{0:T(1024)(128)(4,1)} %bitcast.272), calls=%async_computation.3 | async-start | bytes 1048576
  119.9 6.0 %slice-start.4 = ((s8[4718592]{0:T(1024)(128)(4,1)}), s8[4194304]{0:T(1024)(128)(4,1)S(1)}, s32[]{:S(2)}) async-start(s8[4718592]{0:T(1024)(128)(4,1)} %bitcast.277), calls=%async_computation.4 | async-start | bytes 8388608
  127.4 5.1 %slice-start = ((s8[4718592]{0:T(1024)(128)(4,1)}), s8[4194304]{0:T(1024)(128)(4,1)S(1)}, s32[]{:S(2)}) async-start(s8[4718592]{0:T(1024)(128)(4,1)} %bitcast.269), calls=%async_computation | async-start | bytes 8388608
  128.9 3.6 %slice-start.1 = ((s8[4718592]{0:T(1024)(128)(4,1)}), s8[524288]{0:T(1024)(128)(4,1)S(1)}, s32[]{:S(2)}) async-start(s8[4718592]{0:T(1024)(128)(4,1)} %bitcast.269), calls=%async_computation.1 | async-start | bytes 1048576
  134.0 14.9 %collective-permute-start.2 = (bf16[256,1024]{1,0:T(8,128)(2,1)S(1)}, bf16[256,1024]{1,0:T(8,128)(2,1)S(1)}, u32[]{:S(2)}, u32[]{:S(2)}) collective-permute-start(bf16[256,1024]{1,0:T(8,128)(2,1)S(1)} %fusion.12), channel_id=1, source_target_pairs={{0,1},{1,0},{2,3},{3,2},{4,5},{5,4},{6,7},{7,6},{8,9},{9,8},{10,11... | collective-permute-start | bytes 1572872 | tf_op jit(solution)/shard_map/ppermute | solution.py:101
  139.2 19.6 %collective-permute-start.1 = (bf16[256,1024]{1,0:T(8,128)(2,1)S(1)}, bf16[256,1024]{1,0:T(8,128)(2,1)S(1)}, u32[]{:S(2)}, u32[]{:S(2)}) collective-permute-start(bf16[256,1024]{1,0:T(8,128)(2,1)S(1)} %convolution_convert_fusion.7), channel_id=1, source_target_pairs={{0,1},{1,0},{2,3},{3,2},{4,5},{5,4},{6,7},{7,6},{8,9},{9,8},{10,11... | collective-permute-start | bytes 1572872 | tf_op jit(solution)/shard_map/ppermute | solution.py:101
  143.3 15.5 %copy-start.9 = (bf16[256,1024]{1,0:T(8,128)(2,1)S(1)}, bf16[256,1024]{1,0:T(8,128)(2,1)}, u32[]{:S(2)}) copy-start(bf16[256,1024]{1,0:T(8,128)(2,1)} %param.20) | copy-start | bytes 1572868
  169.7 3.2 copy-start.1
  169.7 3.2 copy-start.36
  171.0 3.4 copy-start.14
  171.0 3.4 copy-start.17
  171.0 3.4 copy-start.26
  171.1 3.4 copy-start.7
  171.1 3.4 copy-start.34
  171.1 3.4 copy-start.42
  171.1 3.5 copy-start.44
  176.6 7.1 %copy-start.43 = (bf16[1024]{0:T(1024)(128)(2,1)S(1)}, bf16[1024]{0:T(1024)(128)(2,1)}, u32[]{:S(2)}) copy-start(bf16[1024]{0:T(1024)(128)(2,1)} %get-tuple-element.100) | copy-start | bytes 6148
  176.6 7.1 %copy-start.10 = (bf16[1024,256]{0,1:T(8,128)(2,1)S(1)}, bf16[1024,256]{0,1:T(8,128)(2,1)}, u32[]{:S(2)}) copy-start(bf16[1024,256]{0,1:T(8,128)(2,1)} %get-tuple-element.104) | copy-start | bytes 1572868
  178.1 14.8 %copy-start.4 = (bf16[256,1024]{1,0:T(8,128)(2,1)}, bf16[256,1024]{1,0:T(8,128)(2,1)S(1)}, u32[]{:S(2)}) copy-start(bf16[256,1024]{1,0:T(8,128)(2,1)S(1)} %fusion.13) | copy-start | bytes 1572868
  178.1 13.0 %collective-permute-start.3 = (bf16[256,1024]{1,0:T(8,128)(2,1)S(1)}, bf16[256,1024]{1,0:T(8,128)(2,1)}, u32[]{:S(2)}, u32[]{:S(2)}) collective-permute-start(bf16[256,1024]{1,0:T(8,128)(2,1)S(1)} %fusion.13), channel_id=1, source_target_pairs={{0,1},{1,0},{2,3},{3,2},{4,5},{5,4},{6,7},{7,6},{8,9},{9,8},{10,11... | collective-permute-start | bytes 1572872 | tf_op jit(solution)/shard_map/ppermute | solution.py:101
  179.9 11.0 %collective-permute-start.4 = (bf16[2,64]{1,0:T(2,128)(2,1)S(1)}, bf16[2,64]{1,0:T(2,128)(2,1)S(1)}, u32[]{:S(2)}, u32[]{:S(2)}) collective-permute-start(bf16[2,64]{1,0:T(2,128)(2,1)S(1)} %pad_maximum_fusion.6), channel_id=1, source_target_pairs={{0,1},{1,0},{2,3},{3,2},{4,5},{5,4},{6,7},{7,6},{8,9},{9,8},{10,11... | collective-permute-start | bytes 776 | tf_op jit(solution)/shard_map/ppermute | solution.py:101
  345.4 4.3 %copy-start.5 = (bf16[256,1024]{1,0:T(8,128)(2,1)S(1)}, bf16[256,1024]{1,0:T(8,128)(2,1)}, u32[]{:S(2)}) copy-start(bf16[256,1024]{1,0:T(8,128)(2,1)} %copy-done.4) | copy-start | bytes 1572868
  (24 other events, 40.0 us)

commit v3 on v2

--- a/solution.py
+++ b/solution.py
@@ -271,13 +271,16 @@
     return [whole.reshape(-1, whole.shape[2]) for whole in wholes]
 
 
-def reduce_kernel(line_size, pieces, *refs):
+def reduce_kernel(line_size, early, pieces, *refs):
+    late = pieces - early
     parts, sums = refs[:pieces], refs[pieces : 2 * pieces]
-    core_bufs = refs[2 * pieces : 3 * pieces]
-    pair_bufs = refs[3 * pieces : 4 * pieces]
-    line_bufs = refs[4 * pieces : 5 * pieces]
-    last_bufs = refs[5 * pieces : 6 * pieces]
-    core_s, core_r, pair_s, pair_r, line_s, line_r, last_r, end_s, end_r = refs[6 * pieces :]
+    line_bufs = refs[2 * pieces : 3 * pieces]
+    last_bufs = refs[3 * pieces : 4 * pieces]
+    core_bufs = refs[4 * pieces : 4 * pieces + late]
+    pair_bufs = refs[4 * pieces + late : 4 * pieces + 2 * late]
+    core_s, core_r, pair_s, pair_r, line_s, line_r, last_r, end_s, end_r = refs[
+        4 * pieces + 2 * late :
+    ]
     replica, index, line, core = place()
     half = replica % 2
     to_core = {"fsdp": index + 1 - 2 * core}
@@ -297,91 +300,109 @@
             pl.when(condition)(copy.start)
         started.append((condition, copy))
 
+    def own_of(p):
+        return parts[p] if p < early else pair_bufs[p - early]
+
+    def meet_cores():
+        for s in order:
+            for q in range(late):
+                full = parts[early + q]
+                arrived = core_bufs[q].at[s]
+                remote(arrived, arrived, core_s.at[s, q], core_r.at[s, q], to_core).wait_recv()
+                core_bufs[q][s, 1 - half] = (
+                    core_bufs[q][s, 1 - half] + full[4 * s + 2 * core + 1 - half]
+                )
+                begin(
+                    None,
+                    remote(
+                        core_bufs[q].at[s, 1 - half],
+                        pair_bufs[q].at[s],
+                        pair_s.at[s, q],
+                        pair_r.at[s, q],
+                        to_pair,
+                    ),
+                )
+                core_bufs[q][s, half] = core_bufs[q][s, half] + full[4 * s + 2 * core + half]
+
+    def along(s, p):
+        own, running = own_of(p), line_bufs[p]
+        if p >= early:
+            q = p - early
+            arrived = own.at[s]
+            remote(arrived, arrived, pair_s.at[s, q], pair_r.at[s, q], to_pair).wait_recv()
+            own[s] = own[s] + core_bufs[q][s, half]
+        opens = jnp.logical_or(
+            jnp.logical_and(line == 0, line < s),
+            jnp.logical_and(line == line_size - 1, line > s),
+        )
+        passes = jnp.logical_or(
+            jnp.logical_and(line > 0, line < s),
+            jnp.logical_and(line < line_size - 1, line > s),
+        )
+
+        @pl.when(passes)
+        def _():
+            arrived = running.at[s]
+            remote(arrived, arrived, line_s.at[s, p], line_r.at[s, p], right).wait_recv()
+            running[s] = running[s] + own[s]
+
+        for condition, source in ((opens, own), (passes, running)):
+            begin(
+                jnp.logical_and(condition, line < s),
+                remote(source.at[s], running.at[s], line_s.at[s, p], line_r.at[s, p], right),
+            )
+            begin(
+                jnp.logical_and(condition, line > s + 1),
+                remote(source.at[s], running.at[s], line_s.at[s, p], line_r.at[s, p], left),
+            )
+            begin(
+                jnp.logical_and(condition, line == s + 1),
+                remote(source.at[s], last_bufs[p], line_s.at[s, p], last_r.at[p], left),
+            )
+
+    def end(s, p):
+        @pl.when(line == s)
+        def _():
+            total = own_of(p)[s]
+            if s > 0:
+                arrived = line_bufs[p].at[s]
+                remote(arrived, arrived, line_s.at[s, p], line_r.at[s, p], right).wait_recv()
+                total = total + line_bufs[p][s]
+            if s < line_size - 1:
+                last = last_bufs[p]
+                remote(last, last, line_s.at[s, p], last_r.at[p], left).wait_recv()
+                total = total + last[...]
+            sums[p][half] = total
+            remote(
+                sums[p].at[half], sums[p].at[half], end_s.at[p], end_r.at[p], to_pair
+            ).start()
+
     greet(replica, index, line, line_size, core)
     for s in order:
-        for p in range(pieces):
+        for q in range(late):
             begin(
                 None,
                 remote(
-                    parts[p].at[pl.ds(4 * s + 2 * (1 - core), 2)],
-                    core_bufs[p].at[s],
-                    core_s.at[s, p],
-                    core_r.at[s, p],
+                    parts[early + q].at[pl.ds(4 * s + 2 * (1 - core), 2)],
+                    core_bufs[q].at[s],
+                    core_s.at[s, q],
+                    core_r.at[s, q],
                     to_core,
                 ),
             )
-    for s in order:
-        for p in range(pieces):
-            arrived = core_bufs[p].at[s]
-            remote(arrived, arrived, core_s.at[s, p], core_r.at[s, p], to_core).wait_recv()
-            core_bufs[p][s, 1 - half] = (
-                core_bufs[p][s, 1 - half] + parts[p][4 * s + 2 * core + 1 - half]
-            )
-            begin(
-                None,
-                remote(
-                    core_bufs[p].at[s, 1 - half],
-                    pair_bufs[p].at[s],
-                    pair_s.at[s, p],
-                    pair_r.at[s, p],
-                    to_pair,
-                ),
-            )
-            core_bufs[p][s, half] = core_bufs[p][s, half] + parts[p][4 * s + 2 * core + half]
-    for s in order:
-        for p in range(pieces):
-            arrived = pair_bufs[p].at[s]
-            remote(arrived, arrived, pair_s.at[s, p], pair_r.at[s, p], to_pair).wait_recv()
-            pair_bufs[p][s] = pair_bufs[p][s] + core_bufs[p][s, half]
-            from_line = line_bufs[p].at[s]
-            passes = jnp.logical_or(
-                jnp.logical_and(line < s, line > 0),
-                jnp.logical_and(line > s, line < line_size - 1),
-            )
-
-            @pl.when(passes)
-            def _(s=s, p=p, from_line=from_line):
-                remote(
-                    from_line, from_line, line_s.at[s, p], line_r.at[s, p], right
-                ).wait_recv()
-                pair_bufs[p][s] = pair_bufs[p][s] + line_bufs[p][s]
-
-            begin(
-                line < s,
-                remote(
-                    pair_bufs[p].at[s], from_line, line_s.at[s, p], line_r.at[s, p], right
-                ),
-            )
-            begin(
-                line > s + 1,
-                remote(pair_bufs[p].at[s], from_line, line_s.at[s, p], line_r.at[s, p], left),
-            )
-            begin(
-                line == s + 1,
-                remote(
-                    pair_bufs[p].at[s], last_bufs[p], line_s.at[s, p], last_r.at[p], left
-                ),
-            )
-    for s in order:
-
-        @pl.when(line == s)
-        def _(s=s):
-            for p in range(pieces):
-                if s > 0:
-                    from_line = line_bufs[p].at[s]
-                    remote(
-                        from_line, from_line, line_s.at[s, p], line_r.at[s, p], right
-                    ).wait_recv()
-                    pair_bufs[p][s] = pair_bufs[p][s] + line_bufs[p][s]
-                if s < line_size - 1:
-                    last = last_bufs[p]
-                    remote(last, last, line_s.at[s, p], last_r.at[p], left).wait_recv()
-                    pair_bufs[p][s] = pair_bufs[p][s] + last[...]
-                sums[p][half] = pair_bufs[p][s]
-                remote(
-                    sums[p].at[half], sums[p].at[half], end_s.at[p], end_r.at[p], to_pair
-                ).start()
-
+    if early:
+        along(order[0], 0)
+    meet_cores()
+    for group in (range(early), range(early, pieces)):
+        for at, s in enumerate(order):
+            for p in group:
+                if at > 0 or p > 0:
+                    along(s, p)
+            if at > 0:
+                for p in group:
+                    end(order[at - 1], p)
+        for p in group:
+            end(order[-1], p)
     for p in range(pieces):
         remote(
             sums[p].at[1 - half], sums[p].at[1 - half], end_s.at[p], end_r.at[p], to_pair
@@ -396,23 +417,48 @@
             pl.when(condition)(copy.wait_send)
 
 
-def reduce_parts(parts):
+def meeting_order(size, rows):
+    core, half = lax.axis_index("fsdp") % 2, lax.axis_index("replica") % 2
+    line_size, half_rows = size // 2, rows // 2
+    at = jnp.arange(size * rows)
+    row, position = at % half_rows, (at // half_rows) % line_size
+    own_half, own_core = (at // (half_rows * line_size)) % 2, at // (2 * half_rows * line_size)
+    from_core = jnp.where(own_core == 1, core, 1 - core)
+    from_half = jnp.where(own_half == 1, half, 1 - half)
+    source = ((2 * position + from_core) * 2 + from_half) * half_rows + row
+    return (jnp.arange(size * rows)[:, None] == source[None, :]).astype(jnp.bfloat16)
+
+
+def meet(left, right):
+    middle = left.shape[1] // 2
+    sent = cross_rows(left[:, :middle], right).astype(jnp.bfloat16)
+    other_core = pair_permute(sent, "fsdp").astype(jnp.float32)
+    mine = (cross_rows(left[:, middle:], right) + other_core).astype(jnp.bfloat16)
+    other_pair = pair_permute(mine[: middle // 2], "replica")
+    both = mine[middle // 2 :].astype(jnp.float32) + other_pair.astype(jnp.float32)
+    return both.astype(jnp.bfloat16)
+
+
+def reduce_parts(met, parts):
     size = lax.axis_size("fsdp")
     line_size = size // 2
-    pieces = len(parts)
-    split = [part.reshape(2 * size, -1, part.shape[1]) for part in parts]
+    early, late = len(met), len(parts)
+    pieces = early + late
+    split = [part.reshape(line_size, -1, part.shape[1]) for part in met]
+    split += [part.reshape(2 * size, -1, part.shape[1]) for part in parts]
     blocks = [part.shape[1:] for part in split]
     kind = jnp.bfloat16
     sums = pl.pallas_call(
-        functools.partial(reduce_kernel, line_size, pieces),
+        functools.partial(reduce_kernel, line_size, early, pieces),
         out_shape=[jax.ShapeDtypeStruct((2,) + block, kind) for block in blocks],
         in_specs=[pl.BlockSpec(memory_space=pltpu.VMEM)] * pieces,
         out_specs=[pl.BlockSpec(memory_space=pltpu.VMEM)] * pieces,
-        scratch_shapes=[pltpu.VMEM((line_size, 2) + block, kind) for block in blocks]
-        + [pltpu.VMEM((line_size,) + block, kind) for block in blocks]
-        + [pltpu.VMEM((line_size,) + block, kind) for block in blocks]
+        scratch_shapes=[pltpu.VMEM((line_size,) + block, kind) for block in blocks]
         + [pltpu.VMEM(block, kind) for block in blocks]
-        + [pltpu.SemaphoreType.DMA((line_size, pieces))] * 6
+        + [pltpu.VMEM((line_size, 2) + block, kind) for block in blocks[early:]]
+        + [pltpu.VMEM((line_size,) + block, kind) for block in blocks[early:]]
+        + [pltpu.SemaphoreType.DMA((line_size, late))] * 4
+        + [pltpu.SemaphoreType.DMA((line_size, pieces))] * 2
         + [pltpu.SemaphoreType.DMA((pieces,))] * 3,
         compiler_params=pltpu.CompilerParams(
             collective_id=1, has_side_effects=True, vmem_limit_bytes=vmem_bytes
@@ -519,11 +565,16 @@
     inner_low = (swish * up_value).astype(jnp.bfloat16)
     swiglu_total = tensor_sum(cross_cols(inner_low, down_full))
     output = (hidden + swiglu_total).astype(jnp.bfloat16)
+    swap = meeting_order(devices, rows)
+    down_met = meet(matmul(cotangent, swap).astype(jnp.bfloat16), inner_low)
     grad_inner = matmul(cotangent, down_full)
     grad_gate = (
         grad_inner * up_value * sigmoid_gate * (1.0 + gate_value * (1.0 - sigmoid_gate))
     ).astype(jnp.bfloat16)
     grad_up = (grad_inner * swish).astype(jnp.bfloat16)
+    second_swapped = matmul(second_low, swap).astype(jnp.bfloat16)
+    gate_met = meet(second_swapped, grad_gate)
+    up_met = meet(second_swapped, grad_up)
     grad_second = tensor_sum(cross_cols(grad_gate, gate_full) + cross_cols(grad_up, up_full))
     second_gain_grad = jnp.sum(grad_second * second_hat, axis=0)
     grad_hidden = cotangent.astype(jnp.float32) + norm_back(
@@ -598,14 +649,7 @@
     attention_part = jnp.concatenate(
         [query_part, key_part, value_part, out_part, small_part], axis=1
     ).astype(jnp.bfloat16)
-    summed = reduce_parts(
-        [
-            cross_rows(second_low, grad_gate).astype(jnp.bfloat16),
-            cross_rows(second_low, grad_up).astype(jnp.bfloat16),
-            cross_rows(cotangent, inner_low).astype(jnp.bfloat16),
-            attention_part,
-        ]
-    )
+    summed = reduce_parts([gate_met, up_met, down_met], [attention_part])
     replicas = lax.axis_size("replica")
     if replicas > 2:
         summed = [lax.psum(total, "replica") * 0.5 for total in summed]

time: 353 us -> 406 us (1.15); the launches traced: 352 us -> 399 us
  waiting for transfers between devices: 26.7 us -> 87.4 us
  Pallas kernels: 225 us -> 192 us
  matrix products: 49.2 us -> 56.7 us
  other arithmetic: 17.5 us -> 22.9 us
    ppermute x5 -> x11, waiting for transfers between devices: 26.7 us -> 87.4 us  [pair_permute(): lax.ppermute(values, axis, [(at, at ^ 1) for at in range(lax.axis_size(ax...]
    pallas_call x1, Pallas kernels: 142 us -> 109 us  [reduce_parts(): pl.pallas_call(functools.partial(reduce_kernel, line_size, early, pieces)...]
    dot_general x7 -> x9, matrix products: 17 us -> 20.6 us  [matmul(): return jnp.dot(left, right, preferred_element_type=jnp.float32)]
    dot_general x7 -> x10, matrix products: 16.5 us -> 20.1 us  [cross_rows(): lax.dot_general(left, right, (((0,), (0,)), ((), ())), preferred_element_...]
    ppermute x5 -> x11, starting transfers between devices: 5.76 us -> 9.16 us  [pair_permute(): lax.ppermute(values, axis, [(at, at ^ 1) for at in range(lax.axis_size(ax...]
    unnamed x118 -> x154, local copies, waits for them, and re-layouts: 11.5 us -> 10.5 us
  transfers between devices with their start and end apart: 5 -> 11, of which waited for: 4 -> 6; matrix products, arithmetic and copies ran while one was open for 6% -> 17% of each run, Pallas kernels for 0% -> 0%
where the time goes in v3:
time: 406 us; the launch traced here: 399 us
  Pallas kernels  192 us (47%)
  waiting for transfers between devices  87.4 us (22%)
  matrix products  56.7 us (14%)
  local copies, waits for them, and re-layouts  28.2 us (7%)
  other arithmetic  22.9 us (6%)
  starting transfers between devices  9.16 us (2%)
    pallas_call x1, Pallas kernels, reduce_parts(): pl.pallas_call(functools.partial(reduce_kernel, line_size, early, pieces)...  109 us
    ppermute x11, waiting for transfers between devices, pair_permute(): lax.ppermute(values, axis, [(at, at ^ 1) for at in range(lax.axis_size(ax...  87.4 us
    pallas_call x1, Pallas kernels, gather_shards(): pl.pallas_call(functools.partial(gather_kernel, line_size, pieces), out_s...  82.9 us
    dot_general x9, matrix products, matmul(): return jnp.dot(left, right, preferred_element_type=jnp.float32)  20.6 us
    dot_general x10, matrix products, cross_rows(): lax.dot_general(left, right, (((0,), (0,)), ((), ())), preferred_element_...  20.1 us
    dot_general x7, matrix products, cross_cols(): lax.dot_general(left, right, (((1,), (1,)), ((), ())), preferred_element_...  11.5 us
    unnamed x154, local copies, waits for them, and re-layouts  10.5 us
    ppermute x11, starting transfers between devices, pair_permute(): lax.ppermute(values, axis, [(at, at ^ 1) for at in range(lax.axis_size(ax...  9.16 us
  transfers between devices with their start and end apart: 11, of which 6 were waited for; matrix products, arithmetic and copies ran while one was open for 17% of the time, Pallas kernels for 0%

profile of v3, /device:TPU:16, one launch (start us, length us, event | category | flops | bytes accessed | tf_op | source)
XLA Modules:
  0.0 398.5 jit_solution(10048567932832849610)
XLA Ops:
  7.4 82.9 %shard_map.204 = (bf16[16,64,1664]{2,1,0:T(8,128)(2,1)}, bf16[16,64,2304]{2,1,0:T(8,128)(2,1)}, bf16[16,64,2304]{2,1,0:T(8,128)(2,1)}, bf16[16,64,2304]{2,1,0:T(8,128)(2,1)}) custom-call(bf16[2,64,1664]{2,1,0:T(8,128)(2,1)} %bitcast.226, bf16[2,64,2304]{2,1,0:T(8,128)(2,1)} %bitcast.233, bf16[2,64,2304]{2,1,0:T(8,128)(2,1)} %bitcast.234, ...), custom_call_target="tpu_custom_call" | custom-call | tf_op jit(solution)/shard_map/pallas_call | solution.py:258
  92.5 1.7 fusion.46
  94.2 1.7 multiply_reduce_fusion.7
  95.9 2.2 convolution_convert_fusion.11
  101.5 2.6 convolution_convert_fusion.8
  104.1 1.5 collective-permute-start
  105.6 1.6 fusion.24
  110.2 3.9 convolution_bitcast_fusion
  114.1 4.6 %collective-permute-done = bf16[256,1024]{1,0:T(8,128)(2,1)} collective-permute-done((bf16[256,1024]{1,0:T(8,128)(2,1)}, bf16[256,1024]{1,0:T(8,128)(2,1)}, u32[]{:S(2)}, u32[]{:S(2)}) %collective-permute-start) | collective-permute-done | bytes 524320 | tf_op jit(solution)/shard_map/ppermute | solution.py:101
  118.7 1.5 multiply_reduce_fusion.2
  121.5 4.1 %fusion.112 = f32[256,2304]{1,0:T(8,128)S(1)} fusion(bf16[256,1024]{1,0:T(8,128)(2,1)S(1)} %multiply_convert_fusion.3, bf16[1024,2304]{1,0:T(8,128)(2,1)} %bitcast.270), kind=kOutput, calls=%fused_computation.224 | convolution fusion | flops 1207959552 | bytes 7602176 | tf_op jit(solution)/shard_map/dot_general | solution.py:45
  125.7 2.1 multiply_convert_fusion
  127.8 1.6 convolution_convert_fusion.7
  129.4 1.6 collective-permute-start.1
  134.6 2.2 convolution_convert_fusion.1
  136.8 2.2 convolution_convert_fusion.2
  139.1 2.2 convolution_convert_fusion
  141.8 12.5 %collective-permute-done.2 = bf16[256,1024]{1,0:T(8,128)(2,1)S(1)} collective-permute-done((bf16[256,1024]{1,0:T(8,128)(2,1)S(1)}, bf16[256,1024]{1,0:T(8,128)(2,1)S(1)}, u32[]{:S(2)}, u32[]{:S(2)}) %collective-permute-start.2) | collective-permute-done | bytes 524320 | tf_op jit(solution)/shard_map/ppermute | solution.py:101
  156.7 2.4 convolution_convert_fusion.9
  171.3 1.5 collective-permute-start.10
  172.9 1.7 fusion.44
  182.9 7.0 %collective-permute-done.3 = bf16[256,1024]{1,0:T(8,128)(2,1)S(1)} collective-permute-done((bf16[256,1024]{1,0:T(8,128)(2,1)S(1)}, bf16[256,1024]{1,0:T(8,128)(2,1)S(1)}, u32[]{:S(2)}, u32[]{:S(2)}) %collective-permute-start.3) | collective-permute-done | bytes 524320 | tf_op jit(solution)/shard_map/ppermute | solution.py:101
  192.4 2.1 copy.97
  195.5 2.3 fusion.21
  197.8 2.6 fusion.16
  200.4 2.6 add_convert_fusion
  205.2 2.5 add_convert_fusion.1
  209.8 2.5 add_convert_fusion.2
  213.3 18.7 %collective-permute-done.9 = bf16[256,2304]{1,0:T(8,128)(2,1)S(1)} collective-permute-done((bf16[256,2304]{1,0:T(8,128)(2,1)S(1)}, bf16[256,2304]{1,0:T(8,128)(2,1)S(1)}, u32[]{:S(2)}, u32[]{:S(2)}) %collective-permute-start.9) | collective-permute-done | bytes 1179680 | tf_op jit(solution)/shard_map/ppermute | solution.py:101
  233.4 24.0 %collective-permute-done.7 = bf16[256,2304]{1,0:T(8,128)(2,1)S(1)} collective-permute-done((bf16[256,2304]{1,0:T(8,128)(2,1)S(1)}, bf16[256,2304]{1,0:T(8,128)(2,1)S(1)}, u32[]{:S(2)}, u32[]{:S(2)}) %collective-permute-start.7) | collective-permute-done | bytes 1179680 | tf_op jit(solution)/shard_map/ppermute | solution.py:101
  258.6 20.6 %collective-permute-done.5 = bf16[256,2304]{1,0:T(8,128)(2,1)S(1)} collective-permute-done((bf16[256,2304]{1,0:T(8,128)(2,1)S(1)}, bf16[256,2304]{1,0:T(8,128)(2,1)S(1)}, u32[]{:S(2)}, u32[]{:S(2)}) %collective-permute-start.5) | collective-permute-done | bytes 1179680 | tf_op jit(solution)/shard_map/ppermute | solution.py:101
  280.5 109.4 %shard_map.205 = (bf16[2,64,2304]{2,1,0:T(8,128)(2,1)}, bf16[2,64,2304]{2,1,0:T(8,128)(2,1)}, bf16[2,64,2304]{2,1,0:T(8,128)(2,1)}, bf16[2,64,1664]{2,1,0:T(8,128)(2,1)}) custom-call(bf16[4,64,2304]{2,1,0:T(8,128)(2,1)} %bitcast.207, bf16[4,64,2304]{2,1,0:T(8,128)(2,1)} %bitcast.206, bf16[4,64,2304]{2,1,0:T(8,128)(2,1)} %bitcast.205, ...), custom_call_target="tpu_custom_call" | custom-call | tf_op jit(solution)/shard_map/pallas_call | solution.py:451
  (263 shorter events, 64.1 us)
Async XLA Ops:
  0.6 5.7 %copy-start.29 = (bf16[2304,128]{1,0:T(8,128)(2,1)S(1)}, bf16[2304,128]{1,0:T(8,128)(2,1)}, u32[]{:S(2)}) copy-start(bf16[2304,128]{1,0:T(8,128)(2,1)} %param.29) | copy-start | bytes 1769476
  6.3 85.9 %copy-start = (bf16[256,1024]{1,0:T(8,128)(2,1)S(1)}, bf16[256,1024]{1,0:T(8,128)(2,1)}, u32[]{:S(2)}) copy-start(bf16[256,1024]{1,0:T(8,128)(2,1)} %param.19) | copy-start | bytes 1572868
  92.4 5.7 %copy-start.52 = (f32[256]{0:T(256)}, f32[256]{0:T(256)S(1)}, u32[]{:S(2)}) copy-start(f32[256]{0:T(256)S(1)} %add_rsqrt_fusion.3) | copy-start | bytes 3076
  94.2 4.2 %copy-start.18 = (f32[256,512]{1,0:T(8,128)}, f32[256,512]{1,0:T(8,128)S(1)}, u32[]{:S(2)}) copy-start(f32[256,512]{1,0:T(8,128)S(1)} %fusion.46) | copy-start | bytes 1572868
  95.9 3.7 copy-start.14
  100.9 4.7 %copy-start.30 = (bf16[256,1024]{1,0:T(8,128)(2,1)S(1)}, bf16[256,1024]{1,0:T(8,128)(2,1)}, u32[]{:S(2)}) copy-start(bf16[256,1024]{1,0:T(8,128)(2,1)} %param.20) | copy-start | bytes 1572868
  101.5 5.7 %copy-start.37 = (bf16[4,64,2,256]{3,1,2,0:T(8,128)(2,1)}, bf16[4,64,2,256]{3,1,2,0:T(8,128)(2,1)S(1)}, u32[]{:S(2)}) copy-start(bf16[4,64,2,256]{3,1,2,0:T(8,128)(2,1)S(1)} %convolution_convert_fusion.10) | copy-start | bytes 786436
  104.1 14.6 %collective-permute-start = (bf16[256,1024]{1,0:T(8,128)(2,1)}, bf16[256,1024]{1,0:T(8,128)(2,1)}, u32[]{:S(2)}, u32[]{:S(2)}) collective-permute-start(bf16[256,1024]{1,0:T(8,128)(2,1)} %convolution_convert_fusion.8), channel_id=1, source_target_pairs={{0,1},{1,0},{2,3},{3,2},{4,5},{5,4},{6,7},{7,6},{8,9},{9,8},{10,11... | collective-permute-start | bytes 1572872 | tf_op jit(solution)/shard_map/ppermute | solution.py:101
  114.1 6.1 %copy-start.43 = (f32[1,1024]{1,0:T(1,128)S(1)}, f32[1,1024]{1,0:T(1,128)}, u32[]{:S(2)}) copy-start(f32[1,1024]{1,0:T(1,128)} %get-tuple-element.135) | copy-start | bytes 12292
  114.1 6.3 %copy-start.62 = (s32[1024]{0:T(1024)S(1)}, s32[1024]{0:T(1024)}, u32[]{:S(2)}) copy-start(s32[1024]{0:T(1024)} %copy-done.61) | copy-start | bytes 12292
  120.4 5.2 %slice-start.2 = ((s8[4718592]{0:T(1024)(128)(4,1)}), s8[4194304]{0:T(1024)(128)(4,1)S(1)}, s32[]{:S(2)}) async-start(s8[4718592]{0:T(1024)(128)(4,1)} %bitcast.274), calls=%async_computation.2 | async-start | bytes 8388608
  121.4 15.4 %copy-start.12 = (bf16[256,1024]{1,0:T(8,128)(2,1)}, bf16[256,1024]{1,0:T(8,128)(2,1)S(1)}, u32[]{:S(2)}) copy-start(bf16[256,1024]{1,0:T(8,128)(2,1)S(1)} %fusion.20) | copy-start | bytes 1572868
  121.4 4.2 %slice-start.3 = ((s8[4718592]{0:T(1024)(128)(4,1)}), s8[524288]{0:T(1024)(128)(4,1)S(1)}, s32[]{:S(2)}) async-start(s8[4718592]{0:T(1024)(128)(4,1)} %bitcast.274), calls=%async_computation.3 | async-start | bytes 1048576
  121.5 6.3 %slice-start.4 = ((s8[4718592]{0:T(1024)(128)(4,1)}), s8[4194304]{0:T(1024)(128)(4,1)S(1)}, s32[]{:S(2)}) async-start(s8[4718592]{0:T(1024)(128)(4,1)} %bitcast.279), calls=%async_computation.4 | async-start | bytes 8388608
  127.8 6.8 %copy-start.6 = (bf16[256,2304]{1,0:T(8,128)(2,1)}, bf16[256,2304]{1,0:T(8,128)(2,1)S(1)}, u32[]{:S(2)}) copy-start(bf16[256,2304]{1,0:T(8,128)(2,1)S(1)} %get-tuple-element.108) | copy-start | bytes 3538948
  127.8 9.1 %copy-start.4 = (bf16[256,2304]{1,0:T(8,128)(2,1)}, bf16[256,2304]{1,0:T(8,128)(2,1)S(1)}, u32[]{:S(2)}) copy-start(bf16[256,2304]{1,0:T(8,128)(2,1)S(1)} %get-tuple-element.109) | copy-start | bytes 3538948
  127.8 11.3 %copy-start.8 = (bf16[256,2304]{1,0:T(8,128)(2,1)}, bf16[256,2304]{1,0:T(8,128)(2,1)S(1)}, u32[]{:S(2)}) copy-start(bf16[256,2304]{1,0:T(8,128)(2,1)S(1)} %get-tuple-element.110) | copy-start | bytes 3538948
  127.8 4.6 %slice-start = ((s8[4718592]{0:T(1024)(128)(4,1)}), s8[4194304]{0:T(1024)(128)(4,1)S(1)}, s32[]{:S(2)}) async-start(s8[4718592]{0:T(1024)(128)(4,1)} %bitcast.271), calls=%async_computation | async-start | bytes 8388608
  129.4 25.8 %collective-permute-start.1 = (bf16[256,1024]{1,0:T(8,128)(2,1)S(1)}, bf16[256,1024]{1,0:T(8,128)(2,1)S(1)}, u32[]{:S(2)}, u32[]{:S(2)}) collective-permute-start(bf16[256,1024]{1,0:T(8,128)(2,1)S(1)} %convolution_convert_fusion.7), channel_id=1, source_target_pairs={{0,1},{1,0},{2,3},{3,2},{4,5},{5,4},{6,7},{7,6},{8,9},{9,8},{10,11... | collective-permute-start | bytes 1572872 | tf_op jit(solution)/shard_map/ppermute | solution.py:101
  133.9 20.4 %collective-permute-start.2 = (bf16[256,1024]{1,0:T(8,128)(2,1)S(1)}, bf16[256,1024]{1,0:T(8,128)(2,1)S(1)}, u32[]{:S(2)}, u32[]{:S(2)}) collective-permute-start(bf16[256,1024]{1,0:T(8,128)(2,1)S(1)} %fusion.22), channel_id=1, source_target_pairs={{0,1},{1,0},{2,3},{3,2},{4,5},{5,4},{6,7},{7,6},{8,9},{9,8},{10,11... | collective-permute-start | bytes 1572872 | tf_op jit(solution)/shard_map/ppermute | solution.py:101
  139.1 16.1 %copy-start.31 = (bf16[256,1024]{1,0:T(8,128)(2,1)S(1)}, bf16[256,1024]{1,0:T(8,128)(2,1)}, u32[]{:S(2)}) copy-start(bf16[256,1024]{1,0:T(8,128)(2,1)} %param.20) | copy-start | bytes 1572868
  141.3 59.1 %collective-permute-start.8 = (bf16[512,2304]{1,0:T(8,128)(2,1)}, bf16[512,2304]{1,0:T(8,128)(2,1)}, u32[]{:S(2)}, u32[]{:S(2)}) collective-permute-start(bf16[512,2304]{1,0:T(8,128)(2,1)} %convolution_convert_fusion), channel_id=1, source_target_pairs={{0,2},{2,0},{4,6},{6,4},{8,10},{10,8},{12,14},{14,12},{1,3},{3,1},... | collective-permute-start | bytes 7077896 | tf_op jit(solution)/shard_map/ppermute | solution.py:101
  141.3 64.0 %collective-permute-start.6 = (bf16[512,2304]{1,0:T(8,128)(2,1)}, bf16[512,2304]{1,0:T(8,128)(2,1)}, u32[]{:S(2)}, u32[]{:S(2)}) collective-permute-start(bf16[512,2304]{1,0:T(8,128)(2,1)} %convolution_convert_fusion.1), channel_id=1, source_target_pairs={{0,2},{2,0},{4,6},{6,4},{8,10},{10,8},{12,14},{14,12},{1,3},{3,1},... | collective-permute-start | bytes 7077896 | tf_op jit(solution)/shard_map/ppermute | solution.py:101
  141.8 68.1 %collective-permute-start.4 = (bf16[512,2304]{1,0:T(8,128)(2,1)}, bf16[512,2304]{1,0:T(8,128)(2,1)}, u32[]{:S(2)}, u32[]{:S(2)}) collective-permute-start(bf16[512,2304]{1,0:T(8,128)(2,1)} %convolution_convert_fusion.2), channel_id=1, source_target_pairs={{0,2},{2,0},{4,6},{6,4},{8,10},{10,8},{12,14},{14,12},{1,3},{3,1},... | collective-permute-start | bytes 7077896 | tf_op jit(solution)/shard_map/ppermute | solution.py:101
  169.4 5.1 %copy-start.34 = (bf16[256,256]{0,1:T(8,128)(2,1)S(1)}, bf16[256,256]{0,1:T(8,128)(2,1)}, u32[]{:S(2)}) copy-start(bf16[256,256]{0,1:T(8,128)(2,1)} %get-tuple-element.126) | copy-start | bytes 393220
  171.3 10.8 %collective-permute-start.10 = (bf16[2,64]{1,0:T(2,128)(2,1)}, bf16[2,64]{1,0:T(2,128)(2,1)}, u32[]{:S(2)}, u32[]{:S(2)}) collective-permute-start(bf16[2,64]{1,0:T(2,128)(2,1)} %pad_maximum_fusion.6), channel_id=1, source_target_pairs={{0,1},{1,0},{2,3},{3,2},{4,5},{5,4},{6,7},{7,6},{8,9},{9,8},{10,11... | collective-permute-start | bytes 776 | tf_op jit(solution)/shard_map/ppermute | solution.py:101
  177.5 12.4 %copy-start.10 = (bf16[256,1024]{1,0:T(8,128)(2,1)}, bf16[256,1024]{1,0:T(8,128)(2,1)S(1)}, u32[]{:S(2)}) copy-start(bf16[256,1024]{1,0:T(8,128)(2,1)S(1)} %fusion.23) | copy-start | bytes 1572868
  177.5 12.4 %collective-permute-start.3 = (bf16[256,1024]{1,0:T(8,128)(2,1)S(1)}, bf16[256,1024]{1,0:T(8,128)(2,1)S(1)}, u32[]{:S(2)}, u32[]{:S(2)}) collective-permute-start(bf16[256,1024]{1,0:T(8,128)(2,1)S(1)} %fusion.23), channel_id=1, source_target_pairs={{0,1},{1,0},{2,3},{3,2},{4,5},{5,4},{6,7},{7,6},{8,9},{9,8},{10,11... | collective-permute-start | bytes 1572872 | tf_op jit(solution)/shard_map/ppermute | solution.py:101
  192.4 8.0 %copy-start.9 = (bf16[256,2304]{1,0:T(8,128)(2,1)S(1)}, bf16[256,2304]{1,0:T(8,128)(2,1)}, u32[]{:S(2)}) copy-start(bf16[256,2304]{1,0:T(8,128)(2,1)} %copy-done.8) | copy-start | bytes 3538948
  203.1 29.0 %collective-permute-start.9 = (bf16[256,2304]{1,0:T(8,128)(2,1)S(1)}, bf16[256,2304]{1,0:T(8,128)(2,1)S(1)}, u32[]{:S(2)}, u32[]{:S(2)}) collective-permute-start(bf16[256,2304]{1,0:T(8,128)(2,1)S(1)} %slice.206), channel_id=1, source_target_pairs={{0,16},{16,0},{1,17},{17,1},{2,18},{18,2},{3,19},{19,3},{4,20},{20... | collective-permute-start | bytes 3538952 | tf_op jit(solution)/shard_map/ppermute | solution.py:101
  207.8 49.5 %collective-permute-start.7 = (bf16[256,2304]{1,0:T(8,128)(2,1)S(1)}, bf16[256,2304]{1,0:T(8,128)(2,1)S(1)}, u32[]{:S(2)}, u32[]{:S(2)}) collective-permute-start(bf16[256,2304]{1,0:T(8,128)(2,1)S(1)} %slice.202), channel_id=1, source_target_pairs={{0,16},{16,0},{1,17},{17,1},{2,18},{18,2},{3,19},{19,3},{4,20},{20... | collective-permute-start | bytes 3538952 | tf_op jit(solution)/shard_map/ppermute | solution.py:101
  212.4 66.8 %collective-permute-start.5 = (bf16[256,2304]{1,0:T(8,128)(2,1)S(1)}, bf16[256,2304]{1,0:T(8,128)(2,1)S(1)}, u32[]{:S(2)}, u32[]{:S(2)}) collective-permute-start(bf16[256,2304]{1,0:T(8,128)(2,1)S(1)} %slice.200), channel_id=1, source_target_pairs={{0,16},{16,0},{1,17},{17,1},{2,18},{18,2},{3,19},{19,3},{4,20},{20... | collective-permute-start | bytes 3538952 | tf_op jit(solution)/shard_map/ppermute | solution.py:101
  (48 other events, 92.5 us)
